TPU v7x, 512 devices: a whole 4x8x8 slice. The times are simulated.
512 devices in a mesh: rows: 32 (over y, x), cols: 16 (over z, core).
Axes of the slice: x: 4, y: 8, z: 8, core: 2. Of those that a mesh axis runs over, the one named last changes fastest.
Arguments:
- source_cells: float32 [64, 32768], P(None, 'rows'), may hold values from -4.5 to 4.5
- target_cells: float32 [64, 32768], P(None, 'cols'), may hold values from -4.5 to 4.5
- source_mass: float32 [32768], P('rows'), may hold values from 0.2 to 15, as said below
- target_mass: float32 [32768], P('cols'), may hold values from 0.2 to 15, as said below
Outputs:
- source_potential: float32 [32768], P('rows')
- target_potential: float32 [32768], P('cols')
- source_map: float32 [64, 32768], P(None, ('rows', 'cols'))
- target_map: float32 [64, 32768], P(None, 'cols')
Inputs may be any that keep to these rules, and one draw needn't show every extreme that they name: `source_mass`: positive weights. `target_mass`: positive weights.
All inputs are finite; a program needn't handle non-finite values.
Results may differ from a plain program's by a relative error of at most 0.0003.
Values sent between devices are 32-bit elements; how exact they have to be, the bound alone decides.
A program may use at most 128 MiB of HBM per device.

v0:
```python
import math

import jax
import jax.numpy as jnp
from jax import lax
from jax.sharding import PartitionSpec as P

ITERS = 2


SMOOTHING = 0.5
PRECISE = lax.Precision.HIGHEST


def cost_block(left_points, right_points, left_norms, right_norms):
    inner = lax.dot_general(
        left_points,
        right_points,
        (((0,), (0,)), ((), ())),
        precision=PRECISE,
        preferred_element_type=jnp.float32,
    )
    return left_norms[:, None] + right_norms[None, :] - 2.0 * inner


def split_blocks(points, block_size):
    features, columns = points.shape
    return points.reshape(features, columns // block_size, block_size).transpose(1, 0, 2)


def join_blocks(stacked):
    return stacked.transpose(1, 0, 2).reshape(stacked.shape[1], -1)


def row_reduce(maximum, summed):
    highest = lax.pmax(maximum, "cols")
    combined = lax.psum(summed * jnp.exp(maximum - highest), "cols")
    return highest + jnp.log(combined)


def column_reduce(maximum, summed):
    highest = lax.pmax(maximum, "rows")
    combined = lax.psum(summed * jnp.exp(maximum - highest), "rows")
    return highest + jnp.log(combined)


def row_partial(source_cells, source_norms, target_cells, target_norms, target_pot, block_size):

    def row_per_block(element):
        points, norms = element
        scores = (
            target_pot[None, :] - cost_block(points, target_cells, norms, target_norms)
        ) / SMOOTHING
        maximum = jnp.max(scores, axis=1)
        return (maximum, jnp.sum(jnp.exp(scores - maximum[:, None]), axis=1))

    maximum, summed = lax.map(
        row_per_block,
        (split_blocks(source_cells, block_size), source_norms.reshape(-1, block_size)),
    )
    return (maximum.reshape(-1), summed.reshape(-1))


def column_partial(source_cells, source_norms, target_cells, target_norms, source_pot, block_size):

    def column_per_block(element):
        points, norms = element
        scores = (
            source_pot[:, None] - cost_block(source_cells, points, source_norms, norms)
        ) / SMOOTHING
        maximum = jnp.max(scores, axis=0)
        weights = jnp.exp(scores - maximum[None, :])
        summed = jnp.sum(weights, axis=0)
        return (maximum, summed)

    outputs = lax.map(
        column_per_block,
        (split_blocks(target_cells, block_size), target_norms.reshape(-1, block_size)),
    )
    return (outputs[0].reshape(-1), outputs[1].reshape(-1))


def project(
    source_cells, source_norms, target_cells, target_norms, source_pot, target_pot, block_size
):
    features = source_cells.shape[0]
    target_count = target_cells.shape[1]

    def project_per_block(running, element):
        points, norms, potential = element
        coupling = jnp.exp(
            (
                potential[:, None]
                + target_pot[None, :]
                - cost_block(points, target_cells, norms, target_norms)
            )
            / SMOOTHING
        )
        numerator = lax.dot_general(
            target_cells,
            coupling,
            (((1,), (1,)), ((), ())),
            precision=PRECISE,
            preferred_element_type=jnp.float32,
        )
        masses = jnp.sum(coupling, axis=1)
        running = (
            running[0]
            + jnp.dot(points, coupling, precision=PRECISE, preferred_element_type=jnp.float32),
            running[1] + jnp.sum(coupling, axis=0),
        )
        return (running, (numerator, masses))

    initial = (
        jnp.zeros((features, target_count), jnp.float32),
        jnp.zeros((target_count,), jnp.float32),
    )
    running, outputs = lax.scan(
        project_per_block,
        initial,
        (
            split_blocks(source_cells, block_size),
            source_norms.reshape(-1, block_size),
            source_pot.reshape(-1, block_size),
        ),
    )
    return (join_blocks(outputs[0]), outputs[1].reshape(-1), running)


def local(source_cells, target_cells, source_mass, target_mass):
    source_sum = lax.psum(jnp.sum(source_mass), "rows")
    target_sum = lax.psum(jnp.sum(target_mass), "cols")
    source_log = jnp.log(source_mass) - jnp.log(source_sum)
    target_log = jnp.log(target_mass) - jnp.log(target_sum)
    source_norms = jnp.sum(source_cells * source_cells, axis=0)
    target_norms = jnp.sum(target_cells * target_cells, axis=0)
    row_block = math.gcd(source_cells.shape[1], 256)
    column_block = math.gcd(target_cells.shape[1], 512)
    target_pot = jnp.zeros((target_cells.shape[1],), jnp.float32)
    for iteration in range(ITERS):
        source_maximum, source_summed = row_partial(
            source_cells, source_norms, target_cells, target_norms, target_pot, row_block
        )
        source_pot = SMOOTHING * source_log - SMOOTHING * row_reduce(source_maximum, source_summed)
        maximum, summed = column_partial(
            source_cells, source_norms, target_cells, target_norms, source_pot, column_block
        )
        target_pot = SMOOTHING * target_log - SMOOTHING * column_reduce(maximum, summed)
    source_numerator, source_masses, running = project(
        source_cells, source_norms, target_cells, target_norms, source_pot, target_pot, row_block
    )
    target_numerator, target_masses = lax.psum((running[0], running[1]), "rows")
    target_map = target_numerator / target_masses[None, :]
    numerator_share, masses_share = (
        lax.psum_scatter(source_numerator, "cols", scatter_dimension=1, tiled=True),
        lax.psum_scatter(source_masses, "cols", scatter_dimension=0, tiled=True),
    )
    source_map = numerator_share / masses_share[None, :]
    return (source_pot, target_pot, source_map, target_map)


def solution(mesh):
    in_specs = (P(None, "rows"), P(None, "cols"), P("rows"), P("cols"))
    out_specs = (P("rows"), P("cols"), P(None, ("rows", "cols")), P(None, "cols"))
    return jax.shard_map(local, mesh=mesh, in_specs=in_specs, out_specs=out_specs, check_vma=False)
```

profile of v0, /device:TPU:1, one launch (start us, length us, event | category | flops | bytes accessed | tf_op | source)
XLA Modules:
  0.0 716.7 jit_solution(2737797503160178395)
XLA Ops:
  8.1 1.0 multiply_reduce_fusion.1
  9.1 1.1 reshape.83
  10.2 1.1 multiply_reduce_fusion
  11.3 1.4 reshape.87
  12.7 0.6 reduce_sum.90
  13.3 62.4 %psum.56 = f32[]{:T(128)} all-reduce(f32[]{:T(128)} %reduce_sum.90), channel_id=1, replica_groups=mesh['rows'=32,'cols'=16] {'rows'}, use_global_device_ids=true, to_apply=%region_1.0 | all-reduce | flops 1 | bytes 8 | tf_op jit(solution)/shard_map/psum | solution.py:131
  76.4 11.3 %while.65 = (s32[]{:T(128)}, f32[4,256]{1,0:T(4,128)S(1)}, f32[4,256]{1,0:T(4,128)S(1)}, f32[4,256]{1,0:T(4,128)S(1)}, f32[2048]{0:T(1024)S(1)}, /*index=5*/f32[...) while((s32[]{:T(128)}, f32[4,256]{1,0:T(4,128)S(1)}, f32[4,256]{1,0:T(4,128)S(1)}, ...), condition=%wide.region_9.10_spmd, body=%wide.region_6.9_spmd.sunk | while | flops 406846976 | bytes 4802677 | solution.py:57
  76.5 2.3 fusion.62
  79.3 2.3 fusion.62
  82.1 2.3 fusion.62
  84.9 2.3 fusion.62
  87.7 44.0 %pmax.28 = f32[1024]{0:T(1024)S(1)} all-reduce(f32[1024]{0:T(1024)S(1)} %bitcast.172), channel_id=1, replica_groups=mesh['rows'=32,'cols'=16] {'cols'}, use_global_device_ids=true, to_apply=%region_10.11 | all-reduce | flops 1024 | bytes 8192 | tf_op jit(solution)/shard_map/pmax | solution.py:36
  131.7 0.6 reduce_sum.91
  132.3 24.1 %all-reduce.1 = (f32[1024]{0:T(1024)S(1)}, f32[]{:T(128)}) all-reduce(f32[1024]{0:T(1024)S(1)} %exponential_multiply_fusion.3, f32[]{:T(128)} %reduce_sum.91), channel_id=1, replica_groups=mesh['rows'=32,'cols'=16] {'cols'}, use_global_device_ids=true, to_apply=%region_11.12 | all-reduce | flops 1025 | bytes 8200 | tf_op jit(solution)/shard_map/psum | solution.py:37
  157.4 11.9 %while.66 = (s32[]{:T(128)}, f32[4,512]{1,0:T(4,128)S(1)}, f32[4,512]{1,0:T(4,128)S(1)}, f32[1024]{0:T(1024)S(1)}, f32[1024]{0:T(1024)S(1)}, /*index=5*/f32[4,51...) while((s32[]{:T(128)}, f32[4,512]{1,0:T(4,128)S(1)}, ...), condition=%wide.region_15.16_spmd, body=%wide.region_12.15_spmd.sunk | while | flops 406846464 | bytes 4616317 | solution.py:76
  157.4 2.3 fusion.64
  159.8 0.5 exponential_reduce_fusion.9
  160.4 2.3 fusion.64
  162.7 0.5 exponential_reduce_fusion.9
  163.4 2.3 fusion.64
  165.7 0.5 exponential_reduce_fusion.9
  166.3 2.3 fusion.64
  168.7 0.5 exponential_reduce_fusion.9
  169.3 56.7 %pmax.29 = f32[2048]{0:T(1024)S(1)} all-reduce(f32[2048]{0:T(1024)S(1)} %bitcast.166), channel_id=1, replica_groups=mesh['rows'=32,'cols'=16] {'rows'}, use_global_device_ids=true, to_apply=%region_16.17 | all-reduce | flops 2048 | bytes 16384 | tf_op jit(solution)/shard_map/pmax | solution.py:42
  226.1 58.8 %psum.59 = f32[2048]{0:T(1024)S(1)} all-reduce(f32[2048]{0:T(1024)S(1)} %exponential_multiply_fusion.1), channel_id=1, replica_groups=mesh['rows'=32,'cols'=16] {'rows'}, use_global_device_ids=true, to_apply=%region_17.18 | all-reduce | flops 2048 | bytes 16384 | tf_op jit(solution)/shard_map/psum | solution.py:43
  284.9 11.4 %while.67 = (s32[]{:T(128)}, f32[4,256]{1,0:T(4,128)S(1)}, f32[4,256]{1,0:T(4,128)S(1)}, f32[2048]{0:T(1024)S(1)}, f32[4,256]{1,0:T(4,128)S(1)}, /*index=5*/f32[...) while((s32[]{:T(128)}, f32[4,256]{1,0:T(4,128)S(1)}, ...), condition=%wide.region_21.22_spmd, body=%wide.region_18.21_spmd.sunk | while | flops 406846976 | bytes 4810877 | solution.py:57
  284.9 2.3 fusion.66
  287.8 2.3 fusion.66
  290.6 2.3 fusion.66
  293.5 2.3 fusion.66
  296.3 51.7 %pmax.30 = f32[1024]{0:T(1024)S(1)} all-reduce(f32[1024]{0:T(1024)S(1)} %bitcast.174), channel_id=1, replica_groups=mesh['rows'=32,'cols'=16] {'cols'}, use_global_device_ids=true, to_apply=%region_22.23 | all-reduce | flops 1024 | bytes 8192 | tf_op jit(solution)/shard_map/pmax | solution.py:36
  348.0 23.5 %psum.60 = f32[1024]{0:T(1024)S(1)} all-reduce(f32[1024]{0:T(1024)S(1)} %exponential_multiply_fusion.2), channel_id=1, replica_groups=mesh['rows'=32,'cols'=16] {'cols'}, use_global_device_ids=true, to_apply=%region_23.24 | all-reduce | flops 1024 | bytes 8192 | tf_op jit(solution)/shard_map/psum | solution.py:37
  371.6 11.9 %while.68 = (s32[]{:T(128)}, f32[4,512]{1,0:T(4,128)S(1)}, f32[4,512]{1,0:T(4,128)S(1)}, f32[1024]{0:T(1024)S(1)}, f32[1024]{0:T(1024)S(1)}, /*index=5*/f32[4,51...) while((s32[]{:T(128)}, f32[4,512]{1,0:T(4,128)S(1)}, ...), condition=%wide.region_27.28_spmd, body=%wide.region_24.27_spmd.sunk | while | flops 406846464 | bytes 4616317 | solution.py:76
  371.6 2.3 fusion.68
  374.0 0.5 exponential_reduce_fusion.11
  374.6 2.3 fusion.68
  376.9 0.5 exponential_reduce_fusion.11
  377.6 2.3 fusion.68
  379.9 0.5 exponential_reduce_fusion.11
  380.6 2.3 fusion.68
  382.9 0.5 exponential_reduce_fusion.11
  383.5 57.2 %pmax.31 = f32[2048]{0:T(1024)S(1)} all-reduce(f32[2048]{0:T(1024)S(1)} %bitcast.168), channel_id=1, replica_groups=mesh['rows'=32,'cols'=16] {'rows'}, use_global_device_ids=true, to_apply=%region_28.29 | all-reduce | flops 2048 | bytes 16384 | tf_op jit(solution)/shard_map/pmax | solution.py:42
  440.8 58.2 %psum.61 = f32[2048]{0:T(1024)S(1)} all-reduce(f32[2048]{0:T(1024)S(1)} %exponential_multiply_fusion), channel_id=1, replica_groups=mesh['rows'=32,'cols'=16] {'rows'}, use_global_device_ids=true, to_apply=%region_29.30 | all-reduce | flops 2048 | bytes 16384 | tf_op jit(solution)/shard_map/psum | solution.py:43
  499.0 27.0 %while.69 = (s32[]{:T(128)}, f32[64,2048]{1,0:T(8,128)S(1)}, f32[2048]{0:T(1024)S(1)}, f32[4,64,256]{2,1,0:T(8,128)}, f32[4,256]{1,0:T(4,128)S(1)}, /*index=5*/f...) while((s32[]{:T(128)}, f32[64,2048]{1,0:T(8,128)S(1)}, ...), condition=%wide.region_33.34_spmd.clone, body=%wide.region_30.33_spmd.clone.sunk | while | flops 1212417792 | bytes 8643748 | solution.py:118
  499.0 2.6 fusion.74
  501.7 2.7 fusion.75
  504.3 1.4 convolution_add_fusion.2
  505.8 2.6 fusion.74
  508.4 2.6 fusion.75
  511.1 1.4 convolution_add_fusion.2
  512.6 2.6 fusion.74
  515.2 2.6 fusion.75
  517.8 1.4 convolution_add_fusion.2
  519.3 2.6 fusion.74
  521.9 2.6 fusion.75
  524.6 1.4 convolution_add_fusion.2
  526.1 2.1 copy.23
  528.8 1.3 dynamic-slice
  530.8 52.3 %all-reduce = f32[1024]{0:T(1024)S(1)} all-reduce(f32[1024]{0:T(1024)S(1)} %bitcast.188), channel_id=3, replica_groups=mesh['rows'=32,'cols'=16] {'cols'}, use_global_device_ids=true, to_apply=%region_35.36.clone | all-reduce | flops 1024 | bytes 8192
  583.2 56.8 %psum.63 = f32[2048]{0:T(1024)S(1)} all-reduce(f32[2048]{0:T(1024)S(1)} %get-tuple-element.242), channel_id=1, replica_groups=mesh['rows'=32,'cols'=16] {'rows'}, use_global_device_ids=true, to_apply=%region_37.38 | all-reduce | flops 2048 | bytes 16384 | tf_op jit(solution)/shard_map/psum | solution.py:152
  639.9 0.8 copy.22
  640.8 0.6 broadcast_divide_fusion.1
  641.4 66.0 %all-reduce.4.cloned.1.call-done = f32[64,2048]{1,0:T(8,128)} async-done(((f32[64,2048]{1,0:T(8,128)}), f32[64,2048]{1,0:T(8,128)}) %all-reduce.4.cloned.1.call-update) | async-done | bytes 524304 | tf_op jit(solution)/shard_map/psum | solution.py:152
  707.4 1.9 broadcast_divide_fusion
  (122 shorter events, 6.4 us)
Async XLA Ops:
  8.0 68.4 %copy-start = (f32[64,2048]{1,0:T(8,128)S(1)}, f32[64,2048]{1,0:T(8,128)}, u32[]{:S(2)}) copy-start(f32[64,2048]{1,0:T(8,128)} %param.15) | copy-start | bytes 1572868
  8.0 4.7 copy-start.4
  8.0 631.9 %reduce-scatter.4.cloned.1.call-start = ((), (), s32[]{:S(2)}) async-start(), calls=%async_computation.2 | async-start | bytes 557056
  76.4 55.3 %copy-start.3 = (f32[2048]{0:T(1024)S(1)}, f32[2048]{0:T(1024)}, u32[]{:S(2)}) copy-start(f32[2048]{0:T(1024)} %param.17) | copy-start | bytes 24580
  76.4 81.0 %copy-start.2 = (f32[64,1024]{1,0:T(8,128)S(1)}, f32[64,1024]{1,0:T(8,128)}, u32[]{:S(2)}) copy-start(f32[64,1024]{1,0:T(8,128)} %param.14) | copy-start | bytes 786436
  383.5 115.5 %copy-start.5 = (f32[1024]{0:T(1024)}, f32[1024]{0:T(1024)S(1)}, u32[]{:S(2)}) copy-start(f32[1024]{0:T(1024)S(1)} %get-tuple-element.921) | copy-start | bytes 12292
  526.0 2.2 copy-start.1
  526.1 183.2 %copy-start.6 = (f32[2048]{0:T(1024)}, f32[2048]{0:T(1024)S(1)}, u32[]{:S(2)}) copy-start(f32[2048]{0:T(1024)S(1)} %get-tuple-element.922) | copy-start | bytes 24580
  528.2 179.2 %all-reduce.4.cloned.1.call-start = ((), (), s32[]{:S(2)}) async-start(), calls=%async_computation.1 | async-start | bytes 1048576 | tf_op jit(solution)/shard_map/psum | solution.py:152
Sparse Core Ops, SparseCore 0:
  528.4 79.4 reduce-scatter.3
Sparse Core Ops, SparseCore 1:
  532.5 174.9 all-reduce.3
where the time goes:
time: 720 us; the launch traced here: 717 us
  blocking collectives  546 us (76%)
  waiting for transfers between devices  66.6 us (9%)
  matrix products  63.5 us (9%)
  between operations  17.8 us (2%)
  other arithmetic  13.6 us (2%)
  local copies, waits for them, and re-layouts  8.9 us (1%)
    psum x2, blocking collectives, column_reduce(): combined = lax.psum(summed * jnp.exp(maximum - highest), 'rows')  117 us
    pmax x2, blocking collectives, column_reduce(): highest = lax.pmax(maximum, 'rows')  114 us
    pmax x2, blocking collectives, row_reduce(): highest = lax.pmax(maximum, 'cols')  95.7 us
    psum x1, waiting for transfers between devices, local(): target_numerator, target_masses = lax.psum((running[0], running[1]), 'rows')  66 us
    psum x1, blocking collectives, local(): source_sum = lax.psum(jnp.sum(source_mass), 'rows')  62.4 us
    psum x1, blocking collectives, local(): target_numerator, target_masses = lax.psum((running[0], running[1]), 'rows')  56.8 us
    unnamed x1, blocking collectives  52.3 us
    psum x2, blocking collectives, row_reduce(): combined = lax.psum(summed * jnp.exp(maximum - highest), 'cols')  47.7 us
  transfers between devices with their start and end apart: 2, of which 1 were waited for; matrix products, arithmetic and copies ran while one was open for 0% of the time, Pallas kernels for 0%

commit v1 on v0

v1 whole, which is shorter than its diff:
```python
import functools
import math

import jax
import jax.numpy as jnp
from jax import lax
from jax.experimental import pallas as pl
from jax.experimental.pallas import tpu as pltpu
from jax.sharding import PartitionSpec as P

MESH = pl.DeviceIdType.MESH
F32 = jnp.float32
BF16 = jnp.bfloat16
LOG2E = math.log2(math.e)
LN2 = math.log(2.0)
NEG = -3.0e38

DIMS = 64
SRC = 1024
TGT = 2048
NX, NY, NZ, NC = 4, 8, 8, 2
GROUPS = 16


def far(n, r):
    return min(r, n - r)


XY_OFFSETS = sorted(
    [(dy, dx) for dy in range(NY) for dx in range(NX) if dy or dx],
    key=lambda o: -(far(NY, o[0]) + far(NX, o[1])),
)
ZC_OFFSETS = sorted(
    [(dz, dc) for dz in range(NZ) for dc in range(NC) if dz or dc],
    key=lambda o: -(far(NZ, o[0]) + 0.3 * o[1]),
)
Y_OFFSETS = sorted(range(1, NY), key=lambda r: -far(NY, r))
X_OFFSETS = sorted(range(1, NX), key=lambda r: -far(NX, r))
Z_OFFSETS = sorted(range(1, NZ), key=lambda r: -far(NZ, r))


def split3(value):
    high = value.astype(BF16)
    rest = value - high.astype(F32)
    middle = rest.astype(BF16)
    low = (rest - middle.astype(F32)).astype(BF16)
    return high, middle, low


def split2(value):
    high = value.astype(BF16)
    return high, (value - high.astype(F32)).astype(BF16)


def fold_rows(value, op):
    rows = value.shape[0]
    while rows > 8:
        rows //= 2
        value = op(value[:rows], value[rows:])
    return value


def to_row(ref, groups):
    return jnp.concatenate([ref[r : r + 1, :] for r in range(groups)], axis=1)


def from_row(ref, value, groups):
    for r in range(groups):
        ref[r : r + 1, :] = value[:, r * 128 : (r + 1) * 128]


def kernel(
    x_ref, y_ref, a_ref, b_ref,
    f_ref, g_ref, smap_ref, tmap_ref,
    xt, yk, t, ehi, elo, fb, part,
    f1_out, f1_in, f2_out, f2_in, g1_out, g1_in, g2_out, g2_in,
    sa_out, sa_in, sb_out, sb_in, row,
    tn, rsx, r1, rsy, r2,
    sn, sc_in, zs, z_in, fin, fin_in,
    send, recv, ag_recv,
):
    rows_at, cols_at = lax.axis_index("rows"), lax.axis_index("cols")
    my, mx = rows_at // NX, lax.rem(rows_at, NX)
    mz, mc = cols_at // NC, lax.rem(cols_at, NC)

    def xy(dy, dx):
        return (lax.rem(my + dy, NY) * NX + lax.rem(mx + dx, NX), cols_at)

    def zc(dz, dc):
        return (rows_at, lax.rem(mz + dz, NZ) * NC + lax.rem(mc + dc, NC))

    def push(src, dst, phase, device, sem=None):
        pltpu.make_async_remote_copy(
            src_ref=src, dst_ref=dst, send_sem=send.at[phase],
            recv_sem=recv.at[phase] if sem is None else sem,
            device_id=device, device_id_type=MESH,
        ).start()

    def await_bytes(ref, sem):
        pltpu.make_async_copy(ref, ref, sem).wait()

    def push_xy(src, slots, phase):
        for dy, dx in XY_OFFSETS:
            push(src, slots.at[dy * NX + dx], phase, xy(dy, dx))

    def push_zc(src, slots, phase):
        for dz, dc in ZC_OFFSETS:
            push(src, slots.at[dz * NC + dc], phase, zc(dz, dc))

    barrier = pltpu.get_barrier_semaphore()
    for dy, dx in XY_OFFSETS:
        pl.semaphore_signal(barrier, inc=1, device_id=xy(dy, dx), device_id_type=MESH)
    for dz, dc in ZC_OFFSETS:
        pl.semaphore_signal(barrier, inc=1, device_id=zc(dz, dc), device_id_type=MESH)

    x = x_ref[...]
    xs = x * (4.0 * LOG2E)
    xh, xm, xl = split3(xs)
    xt[:, 0:128] = jnp.concatenate([xh.astype(F32), xm.astype(F32)], axis=0).T.astype(BF16)
    xt[:, 128:256] = xt[:, 0:128]
    xt[:, 256:384] = jnp.concatenate([xh.astype(F32), xl.astype(F32)], axis=0).T.astype(BF16)
    xt[:, 384:512] = jnp.where(lax.broadcasted_iota(jnp.int32, (SRC, 128), 1) < 3, 1.0, 0.0).astype(BF16)
    y = y_ref[...]
    yh, ym, yl = split3(y)
    yk[0:64, :] = yh
    yk[64:128, :] = yh
    yk[128:192, :] = ym
    yk[192:256, :] = ym
    yk[256:320, :] = yl
    yk[320:384, :] = yh
    ny = jnp.sum(y * y, axis=0, keepdims=True) * (-2.0 * LOG2E)
    nh, nm, nl = split3(ny)
    pick = lax.broadcasted_iota(jnp.int32, (128, TGT), 0)
    norms = jnp.where(
        pick == 0, nh.astype(F32), jnp.where(pick == 1, nm.astype(F32), jnp.where(pick == 2, nl.astype(F32), 0.0))
    )
    yk[384:512, :] = norms.astype(BF16)

    def first(k, _):
        at = pl.ds(pl.multiple_of(k * 128, 128), 128)
        t[at, :] = jnp.dot(xt[at, :], yk[...], preferred_element_type=F32)
        highest = t[at, 0:128]
        for g in range(1, GROUPS):
            highest = jnp.maximum(highest, t[at, g * 128 : (g + 1) * 128])
        total = jnp.exp2(t[at, 0:128] - highest)
        for g in range(1, GROUPS):
            total += jnp.exp2(t[at, g * 128 : (g + 1) * 128] - highest)
        highest, total = highest.T, total.T
        top = jnp.max(highest, axis=0, keepdims=True)
        summed = jnp.sum(total * jnp.exp2(highest - top), axis=0, keepdims=True)
        f1_out[pl.ds(k, 1), :] = top + jnp.log(summed) * LOG2E
        return 0

    lax.fori_loop(0, 8, first, 0)
    sa_out[...] = jnp.broadcast_to(jnp.sum(a_ref[...], axis=(0, 1), keepdims=True), (1, 128))
    sb_out[...] = jnp.broadcast_to(jnp.sum(b_ref[...], axis=(0, 1), keepdims=True), (1, 128))

    pl.semaphore_wait(barrier, len(XY_OFFSETS) + len(ZC_OFFSETS))
    push_zc(f1_out, f1_in, 0)
    push_xy(sa_out, sa_in, 1)
    push_zc(sb_out, sb_in, 2)

    f1_in[0] = f1_out[...]
    await_bytes(f1_in.at[pl.ds(1, 15)], recv.at[0])
    highest = jnp.max(f1_in[...], axis=0)
    summed = jnp.sum(jnp.exp2(f1_in[...] - highest[None]), axis=0)
    log_a = jnp.log(a_ref[...]) * LOG2E
    first_f = log_a - (highest + jnp.log(summed) * LOG2E)
    row[0:8, :] = first_f
    for r in range(8):
        fb[r * 128 : (r + 1) * 128, :] = jnp.broadcast_to(row[r : r + 1, :], (128, 128)).T

    WIDE = 512
    for c in range(TGT // WIDE):
        cs = slice(c * WIDE, (c + 1) * WIDE)

        def shifted(k, top):
            at = pl.ds(pl.multiple_of(k * 64, 64), 64)
            f = fb[at, :]
            value = t[at, cs] + jnp.concatenate([f] * (WIDE // 128), axis=1)
            t[at, cs] = value
            return jnp.maximum(top, fold_rows(value, jnp.maximum))

        top = lax.fori_loop(0, 16, shifted, jnp.full((8, WIDE), NEG, F32), unroll=2)
        top = jnp.max(top, axis=0, keepdims=True)

        def powers(k, total):
            at = pl.ds(pl.multiple_of(k * 64, 64), 64)
            e = jnp.exp2(t[at, cs] - top)
            t[at, cs] = e
            high, low = split2(e)
            ehi[at, cs] = high
            elo[at, cs] = low
            return total + fold_rows(e, jnp.add)

        total = lax.fori_loop(0, 16, powers, jnp.zeros((8, WIDE), F32), unroll=2)
        total = jnp.sum(total, axis=0, keepdims=True)
        logs = top + jnp.log(total) * LOG2E
        for r in range(WIDE // 128):
            at = c * (WIDE // 128) + r
            g1_out[at : at + 1, :] = logs[:, r * 128 : (r + 1) * 128]
            row[8 + at : 9 + at, :] = top[:, r * 128 : (r + 1) * 128]
    push_xy(g1_out, g1_in, 3)
    g1_in[0] = g1_out[...]
    await_bytes(g1_in.at[pl.ds(1, 31)], recv.at[3])
    highest = jnp.max(g1_in[...], axis=0)
    summed = jnp.sum(jnp.exp2(g1_in[...] - highest[None]), axis=0)
    b = b_ref[...]
    first_g = jnp.log(b) * LOG2E - (highest + jnp.log(summed) * LOG2E)
    row[8:24, :] = jnp.exp2(row[8:24, :] + first_g)
    scale = to_row(row.at[8:24, :], 16)

    def weighted(k, _):
        at = pl.ds(pl.multiple_of(k * 64, 64), 64)
        total = t[at, 0:128] * scale[:, 0:128]
        for g in range(1, GROUPS):
            gs = slice(g * 128, (g + 1) * 128)
            total += t[at, gs] * scale[:, gs]
        part[at, :] = total
        return 0

    lax.fori_loop(0, 16, weighted, 0, unroll=2)
    for r in range(8):
        f2_out[r : r + 1, :] = jnp.sum(part[r * 128 : (r + 1) * 128, :].T, axis=0, keepdims=True)
    push_zc(f2_out, f2_in, 4)
    f2_in[0] = f2_out[...]
    nx = jnp.sum(x * x, axis=0, keepdims=True) * (2.0 * LOG2E)
    from_row(row.at[24:32, :], nx, 8)
    await_bytes(f2_in.at[pl.ds(1, 15)], recv.at[4])
    sums = jnp.sum(f2_in[...], axis=0)
    ratio = a_ref[...] / sums
    row[32:40, :] = ratio
    u = to_row(row.at[32:40, :], 8)

    def stacked(points, weights):
        high, low = split2(points * weights)
        wh, wl = split2(weights)
        tail = lax.broadcasted_iota(jnp.int32, (16, weights.shape[1]), 0)
        pair = jnp.where(tail == 0, wh.astype(F32), jnp.where(tail == 1, wl.astype(F32), 0.0))
        return jnp.concatenate([high, low, pair.astype(BF16)], axis=0)

    xu = stacked(x, u)
    for c in range(4):
        cs = slice(c * 512, (c + 1) * 512)
        one = jnp.dot(xu, ehi[:, cs], preferred_element_type=F32)
        two = jnp.dot(xu, elo[:, cs], preferred_element_type=F32)
        w = scale[:, cs]
        tn[:, cs] = (one[0:64] + one[64:128] + two[0:64]) * w
        mass = (one[128:129] + one[129:130] + two[128:129]) * w
        for r in range(4):
            g2_out[c * 4 + r : c * 4 + r + 1, :] = mass[:, r * 128 : (r + 1) * 128]
    push_xy(g2_out, g2_in, 5)
    for dx in X_OFFSETS:
        at = pl.multiple_of(lax.rem(mx + dx, NX) * 512, 512)
        push(tn.at[:, pl.ds(at, 512)], rsx.at[dx], 6, xy(0, dx))
    g2_in[0] = g2_out[...]
    await_bytes(g2_in.at[pl.ds(1, 31)], recv.at[5])
    mass = jnp.sum(g2_in[...], axis=0)
    ratio_g = b / mass
    row[40:56, :] = row[8:24, :] * ratio_g
    row[56:72, :] = mass
    q = to_row(row.at[40:56, :], 16)

    await_bytes(rsx.at[pl.ds(1, 3)], recv.at[6])
    own = pl.ds(pl.multiple_of(mx * 512, 512), 512)
    r1[...] = tn[:, own] + rsx[1] + rsx[2] + rsx[3]

    def y_piece(position):
        half, group = lax.rem(position, 2), position // 2
        return (
            pl.ds(pl.multiple_of(half * 32, 32), 32),
            pl.ds(pl.multiple_of(group * 128, 128), 128),
        )

    for dy in Y_OFFSETS:
        halves, groups = y_piece(lax.rem(my + dy, NY))
        push(r1.at[halves, groups], rsy.at[dy], 7, xy(dy, 0))

    yq = stacked(y, q)
    nt = (((1,), (1,)), ((), ()))
    for c in range(4):
        rs = slice(c * 256, (c + 1) * 256)
        one = lax.dot_general(yq, ehi[rs, :], nt, preferred_element_type=F32)
        two = lax.dot_general(yq, elo[rs, :], nt, preferred_element_type=F32)
        sn[0, :, rs] = one[0:32] + one[64:96] + two[0:32]
        sn[1, :, rs] = one[32:64] + one[96:128] + two[32:64]
        weight = one[128:129] + one[129:130] + two[128:129]
        sn[2, :, rs] = jnp.broadcast_to(weight, (32, 256))
    partner = zc(0, 1)
    push(sn.at[1 - mc], sc_in.at[pl.ds(0, 32)], 8, partner)
    push(sn.at[2, pl.ds(0, 8)], sc_in.at[pl.ds(32, 8)], 8, partner)
    await_bytes(sc_in, recv.at[8])
    for k in range(NZ):
        ks = slice(k * 128, (k + 1) * 128)
        zs[k, 0:32, :] = sn[mc, :, ks] + sc_in[0:32, ks]
        zs[k, 32:40, :] = sn[2, 0:8, ks] + sc_in[32:40, ks]
    for dz in Z_OFFSETS:
        push(zs.at[lax.rem(mz + dz, NZ)], z_in.at[dz], 9, zc(dz, 0))

    await_bytes(rsy.at[pl.ds(1, 7)], recv.at[7])
    halves, groups = y_piece(my)
    own_sum = r1[halves, groups]
    for k in range(1, NY):
        own_sum += rsy[k]
    mass_at = 56 + mx * 4 + my // 2
    r2[...] = own_sum / row[pl.ds(mass_at, 1), :]
    out_rows = halves
    out_cols = pl.ds(pl.multiple_of(mx * 512 + (my // 2) * 128, 128), 128)
    for dy in Y_OFFSETS:
        push(r2, tmap_ref.at[out_rows, out_cols], 10, xy(dy, 0))
    tmap_ref[out_rows, out_cols] = r2[...]

    await_bytes(z_in.at[pl.ds(1, 7)], recv.at[9])
    own_sum = zs[mz]
    for k in range(1, NZ):
        own_sum += z_in[k]
    fin[...] = own_sum[0:32] / own_sum[32:33]
    push(fin, fin_in, 11, partner)

    await_bytes(rsy.at[pl.ds(1, 7)], recv.at[10])
    for dx in X_OFFSETS:
        push(tmap_ref.at[:, own], tmap_ref.at[:, own], 12, xy(0, dx))

    sa_in[0] = sa_out[...]
    sb_in[0] = sb_out[...]
    await_bytes(sa_in.at[pl.ds(1, 31)], recv.at[1])
    await_bytes(sb_in.at[pl.ds(1, 15)], recv.at[2])
    log_sa = jnp.log(jnp.sum(sa_in[...], axis=0))
    log_sb = jnp.log(jnp.sum(sb_in[...], axis=0))
    f_ref[...] = (0.5 * LN2) * (first_f + row[24:32, :]) + 0.5 * jnp.log(ratio) - (log_sa - 0.5 * log_sb)
    g_ref[...] = (0.5 * LN2) * first_g + 0.5 * jnp.log(ratio_g) - (log_sb - log_sa)

    await_bytes(fin_in, recv.at[11])
    mine, other = fin[...], fin_in[...]
    low = jnp.where(mc == 0, mine, other)
    high = jnp.where(mc == 0, other, mine)
    both = jnp.concatenate([low, high], axis=0)
    smap_ref[...] = jnp.where(mc == 0, both[:, 0:64], both[:, 64:128])

    await_bytes(rsx.at[pl.ds(1, 3)], recv.at[12])

    await_bytes(f1_in.at[pl.ds(1, 15)], send.at[0])
    await_bytes(sa_in.at[pl.ds(1, 31)], send.at[1])
    await_bytes(sb_in.at[pl.ds(1, 15)], send.at[2])
    await_bytes(g1_in.at[pl.ds(1, 31)], send.at[3])
    await_bytes(f2_in.at[pl.ds(1, 15)], send.at[4])
    await_bytes(g2_in.at[pl.ds(1, 31)], send.at[5])
    await_bytes(rsx.at[pl.ds(1, 3)], send.at[6])
    await_bytes(rsy.at[pl.ds(1, 7)], send.at[7])
    await_bytes(sc_in, send.at[8])
    await_bytes(z_in.at[pl.ds(1, 7)], send.at[9])
    await_bytes(rsy.at[pl.ds(1, 7)], send.at[10])
    await_bytes(fin_in, send.at[11])
    await_bytes(rsx.at[pl.ds(1, 3)], send.at[12])


def local(source_cells, target_cells, source_mass, target_mass):
    vmem = pl.BlockSpec(memory_space=pltpu.VMEM)
    f, g, smap, tmap = pl.pallas_call(
        kernel,
        out_shape=(
            jax.ShapeDtypeStruct((8, 128), F32),
            jax.ShapeDtypeStruct((16, 128), F32),
            jax.ShapeDtypeStruct((DIMS, 64), F32),
            jax.ShapeDtypeStruct((DIMS, TGT), F32),
        ),
        in_specs=[vmem] * 4,
        out_specs=(vmem,) * 4,
        scratch_shapes=[
            pltpu.VMEM((SRC, 512), BF16),
            pltpu.VMEM((512, TGT), BF16),
            pltpu.VMEM((SRC, TGT), F32),
            pltpu.VMEM((SRC, TGT), BF16),
            pltpu.VMEM((SRC, TGT), BF16),
            pltpu.VMEM((SRC, 128), F32),
            pltpu.VMEM((SRC, 128), F32),
            pltpu.VMEM((8, 128), F32),
            pltpu.VMEM((16, 8, 128), F32),
            pltpu.VMEM((8, 128), F32),
            pltpu.VMEM((16, 8, 128), F32),
            pltpu.VMEM((16, 128), F32),
            pltpu.VMEM((32, 16, 128), F32),
            pltpu.VMEM((16, 128), F32),
            pltpu.VMEM((32, 16, 128), F32),
            pltpu.VMEM((1, 128), F32),
            pltpu.VMEM((32, 1, 128), F32),
            pltpu.VMEM((1, 128), F32),
            pltpu.VMEM((16, 1, 128), F32),
            pltpu.VMEM((72, 128), F32),
            pltpu.VMEM((DIMS, TGT), F32),
            pltpu.VMEM((NX, DIMS, 512), F32),
            pltpu.VMEM((DIMS, 512), F32),
            pltpu.VMEM((NY, 32, 128), F32),
            pltpu.VMEM((32, 128), F32),
            pltpu.VMEM((3, 32, SRC), F32),
            pltpu.VMEM((40, SRC), F32),
            pltpu.VMEM((NZ, 40, 128), F32),
            pltpu.VMEM((NZ, 40, 128), F32),
            pltpu.VMEM((32, 128), F32),
            pltpu.VMEM((32, 128), F32),
            pltpu.SemaphoreType.DMA((13,)),
            pltpu.SemaphoreType.DMA((13,)),
            pltpu.SemaphoreType.DMA((8,)),
        ],
        compiler_params=pltpu.CompilerParams(
            collective_id=0, has_side_effects=True, vmem_limit_bytes=56 << 20
        ),
    )(source_cells, target_cells, source_mass.reshape(8, 128), target_mass.reshape(16, 128))
    return f.reshape(-1), g.reshape(-1), smap, tmap


def solution(mesh):
    in_specs = (P(None, "rows"), P(None, "cols"), P("rows"), P("cols"))
    out_specs = (P("rows"), P("cols"), P(None, ("rows", "cols")), P(None, "cols"))
    return jax.shard_map(local, mesh=mesh, in_specs=in_specs, out_specs=out_specs, check_vma=False)
```

time: 720 us -> 79 us (0.11)
  blocking collectives: 546 us -> 0 us
  Pallas kernels: 0 us -> 73 us
  waiting for transfers between devices: 66.6 us -> 0 us
  matrix products: 63.5 us -> 0 us
  between operations: 17.8 us -> 0.65 us
  other arithmetic: 13.6 us -> 0 us
    psum x6 -> x0, blocking collectives: 284 us -> none  [the longest x2 117 us: column_reduce(): combined = lax.psum(summed * jnp.exp(maximum - highest), 'rows')]
    pmax x4 -> x0, blocking collectives: 210 us -> none  [the longest x2 114 us: column_reduce(): highest = lax.pmax(maximum, 'rows')]
    pallas_call x0 -> x1, Pallas kernels: none -> 73 us  [local(): pl.pallas_call(kernel, out_shape=(jax.ShapeDtypeStruct((8, 128), F32), ja...]
    psum x1 -> x0, waiting for transfers between devices: 66 us -> none  [local(): target_numerator, target_masses = lax.psum((running[0], running[1]), 'rows')]
    dot_general x28 -> x0, matrix products: 63.5 us -> none  [the longest x20 47.2 us: cost_block(): lax.dot_general(left_points, right_points, (((0,), (0,)), ((), ())), prec...]
    unnamed x1 -> x0, blocking collectives: 52.3 us -> none
    reduce_sum x20 -> x0, other arithmetic: 10.9 us -> none  [the longest x8 4.12 us: column_per_block(): summed = jnp.sum(weights, axis=0)]
  transfers between devices with their start and end apart: 2 -> 0, of which waited for: 1 -> 0; matrix products, arithmetic and copies ran while one was open for 0% -> 0% of each run, Pallas kernels for 0% -> 0%
where the time goes in v1:
time: 79 us; the launch traced here: 78.7 us
  Pallas kernels  73 us (92%)
  local copies, waits for them, and re-layouts  5.06 us (6%)
    pallas_call x1, Pallas kernels, local(): pl.pallas_call(kernel, out_shape=(jax.ShapeDtypeStruct((8, 128), F32), ja...  73 us
    unnamed x6, local copies, waits for them, and re-layouts  5.06 us

profile of v1, /device:TPU:1, one launch (start us, length us, event | category | flops | bytes accessed | tf_op | source)
XLA Modules:
  0.0 78.7 jit_solution(10771876785929383378)
XLA Ops:
  0.6 73.0 %shard_map.75 = (f32[8,128]{1,0:T(8,128)}, f32[16,128]{1,0:T(8,128)}, f32[64,64]{1,0:T(8,128)}, f32[64,2048]{1,0:T(8,128)}) custom-call(f32[64,1024]{1,0:T(8,128)} %x_ref.1, f32[64,2048]{1,0:T(8,128)} %y_ref.1, f32[8,128]{1,0:T(8,128)} %bitcast.6, f32[16,128]{1,0:T(8,128)} %bitcast.4), custom_call_target="tpu_custom_call" | custom-call | tf_op jit(solution)/shard_map/pallas_call | solution.py:359
  73.6 0.0 copy-start
  73.6 1.3 %copy.12 = f32[1024]{0:T(1024)} copy(f32[1024]{0:T(1024)} %bitcast.7) | data formatting | bytes 8192
  74.9 1.3 %copy.13 = f32[2048]{0:T(1024)} copy(f32[2048]{0:T(1024)} %bitcast.5) | data formatting | bytes 16384
  76.2 0.0 copy-done
  76.2 0.6 copy.14
  76.8 1.9 %copy.15 = f32[64,2048]{1,0:T(8,128)} copy(f32[64,2048]{1,0:T(8,128)} %get-tuple-element.19) | data formatting | bytes 1048576
Async XLA Ops:
  73.6 2.6 %copy-start = (f32[64,64]{1,0:T(8,128)S(1)}, f32[64,64]{1,0:T(8,128)}, u32[]{:S(2)}) copy-start(f32[64,64]{1,0:T(8,128)} %get-tuple-element.18) | copy-start | bytes 49156

commit v2 on v1

v2 whole, which is shorter than its diff:
```python
import functools
import math

import jax
import jax.numpy as jnp
from jax import lax
from jax.experimental import pallas as pl
from jax.experimental.pallas import tpu as pltpu
from jax.sharding import PartitionSpec as P

MESH = pl.DeviceIdType.MESH
F32 = jnp.float32
BF16 = jnp.bfloat16
LOG2E = math.log2(math.e)
LN2 = math.log(2.0)
NEG = -3.0e38

DIMS = 64
SRC = 1024
TGT = 2048
NX, NY, NZ, NC = 4, 8, 8, 2
GROUPS = 16


def far(n, r):
    return min(r, n - r)


XY_OFFSETS = sorted(
    [(dy, dx) for dy in range(NY) for dx in range(NX) if dy or dx],
    key=lambda o: -(far(NY, o[0]) + far(NX, o[1])),
)
ZC_OFFSETS = sorted(
    [(dz, dc) for dz in range(NZ) for dc in range(NC) if dz or dc],
    key=lambda o: -(far(NZ, o[0]) + 0.3 * o[1]),
)
Y_OFFSETS = sorted(range(1, NY), key=lambda r: -far(NY, r))
X_OFFSETS = sorted(range(1, NX), key=lambda r: -far(NX, r))
Z_OFFSETS = sorted(range(1, NZ), key=lambda r: -far(NZ, r))


def split3(value):
    high = value.astype(BF16)
    rest = value - high.astype(F32)
    middle = rest.astype(BF16)
    low = (rest - middle.astype(F32)).astype(BF16)
    return high, middle, low


def split2(value):
    high = value.astype(BF16)
    return high, (value - high.astype(F32)).astype(BF16)


def fold_rows(value, op):
    rows = value.shape[0]
    while rows > 8:
        rows //= 2
        value = op(value[:rows], value[rows:])
    return value


def to_row(ref, groups):
    return jnp.concatenate([ref[r : r + 1, :] for r in range(groups)], axis=1)


def from_row(ref, value, groups):
    for r in range(groups):
        ref[r : r + 1, :] = value[:, r * 128 : (r + 1) * 128]


def kernel(
    x_hbm, y_hbm, a_hbm, b_hbm,
    fg_hbm, smap_hbm, tmap_hbm,
    x_ref, y_ref, a_ref, b_ref, fg_ref, smap_ref, ta_ref, tb_ref,
    xt, yk, t, ehi, elo, fb, part,
    f1_out, f1_in, f2_out, f2_in, g1_out, g1a_in, g1b_in, g2_out, g2a_in, g2b_in,
    sa_out, sa_in, sb_out, sb_in, row,
    na, nb, ax_in, ra, ay_in, by_in, rb, bx_in, fin_t,
    sn, sc_in, zs, z_in, fin, fin_in,
    send, recv, near,
):
    rows_at, cols_at = lax.axis_index("rows"), lax.axis_index("cols")
    my, mx = rows_at // NX, lax.rem(rows_at, NX)
    mz, mc = cols_at // NC, lax.rem(cols_at, NC)

    def xy(dy, dx):
        return (lax.rem(my + dy, NY) * NX + lax.rem(mx + dx, NX), cols_at)

    def zc(dz, dc):
        return (rows_at, lax.rem(mz + dz, NZ) * NC + lax.rem(mc + dc, NC))

    def push(src, dst, phase, device):
        pltpu.make_async_remote_copy(
            src_ref=src, dst_ref=dst, send_sem=send.at[phase], recv_sem=recv.at[phase],
            device_id=device, device_id_type=MESH,
        ).start()

    def await_bytes(ref, sem):
        pltpu.make_async_copy(ref, ref, sem).wait()

    def push_xy(src, slots, phase):
        for dy, dx in XY_OFFSETS:
            push(src, slots.at[dy * NX + dx], phase, xy(dy, dx))

    def push_zc(src, slots, phase):
        for dz, dc in ZC_OFFSETS:
            push(src, slots.at[dz * NC + dc], phase, zc(dz, dc))

    def fetch(src, dst, k):
        copy = pltpu.make_async_copy(src, dst, near.at[k])
        copy.start()
        return copy

    loads = [
        fetch(x_hbm, x_ref, 0),
        fetch(y_hbm, y_ref, 1),
        fetch(a_hbm, a_ref, 2),
        fetch(b_hbm, b_ref, 3),
    ]
    barrier = pltpu.get_barrier_semaphore()
    for dy, dx in XY_OFFSETS:
        pl.semaphore_signal(barrier, inc=1, device_id=xy(dy, dx), device_id_type=MESH)
    for dz, dc in ZC_OFFSETS:
        pl.semaphore_signal(barrier, inc=1, device_id=zc(dz, dc), device_id_type=MESH)

    loads[0].wait()
    x = x_ref[...]
    xs = x * (4.0 * LOG2E)
    xh, xm, xl = split3(xs)
    xt[:, 0:128] = jnp.concatenate([xh.astype(F32), xm.astype(F32)], axis=0).T.astype(BF16)
    xt[:, 128:256] = xt[:, 0:128]
    xt[:, 256:384] = jnp.concatenate([xh.astype(F32), xl.astype(F32)], axis=0).T.astype(BF16)
    xt[:, 384:512] = jnp.where(lax.broadcasted_iota(jnp.int32, (SRC, 128), 1) < 3, 1.0, 0.0).astype(BF16)
    loads[1].wait()
    y = y_ref[...]
    yh, ym, yl = split3(y)
    yk[0:64, :] = yh
    yk[64:128, :] = yh
    yk[128:192, :] = ym
    yk[192:256, :] = ym
    yk[256:320, :] = yl
    yk[320:384, :] = yh
    ny = jnp.sum(y * y, axis=0, keepdims=True) * (-2.0 * LOG2E)
    nh, nm, nl = split3(ny)
    pick = lax.broadcasted_iota(jnp.int32, (16, TGT), 0)
    norms = jnp.where(
        pick == 0, nh.astype(F32), jnp.where(pick == 1, nm.astype(F32), jnp.where(pick == 2, nl.astype(F32), 0.0))
    )
    yk[384:400, :] = norms.astype(BF16)
    yk[400:512, :] = jnp.zeros((112, TGT), BF16)

    def score(k):
        at = slice(k * 128, (k + 1) * 128)
        t[at, :] = jnp.dot(xt[at, :], yk[...], preferred_element_type=F32)

    def row_logs(k):
        at = slice(k * 128, (k + 1) * 128)
        highest = t[at, 0:128]
        for g in range(1, GROUPS):
            highest = jnp.maximum(highest, t[at, g * 128 : (g + 1) * 128])
        total = jnp.exp2(t[at, 0:128] - highest)
        for g in range(1, GROUPS):
            total += jnp.exp2(t[at, g * 128 : (g + 1) * 128] - highest)
        highest, total = highest.T, total.T
        top = jnp.max(highest, axis=0, keepdims=True)
        summed = jnp.sum(total * jnp.exp2(highest - top), axis=0, keepdims=True)
        f1_out[k : k + 1, :] = top + jnp.log(summed) * LOG2E

    score(0)
    for k in range(8):
        if k < 7:
            score(k + 1)
        row_logs(k)
    loads[2].wait()
    loads[3].wait()
    sa_out[...] = jnp.broadcast_to(jnp.sum(a_ref[...], axis=(0, 1), keepdims=True), (1, 128))
    sb_out[...] = jnp.broadcast_to(jnp.sum(b_ref[...], axis=(0, 1), keepdims=True), (1, 128))

    pl.semaphore_wait(barrier, len(XY_OFFSETS) + len(ZC_OFFSETS))
    push_zc(f1_out, f1_in, 0)
    push_xy(sa_out, sa_in, 1)
    push_zc(sb_out, sb_in, 2)

    f1_in[0] = f1_out[...]
    await_bytes(f1_in.at[pl.ds(1, 15)], recv.at[0])
    highest = jnp.max(f1_in[...], axis=0)
    summed = jnp.sum(jnp.exp2(f1_in[...] - highest[None]), axis=0)
    log_a = jnp.log(a_ref[...]) * LOG2E
    first_f = log_a - (highest + jnp.log(summed) * LOG2E)
    row[0:8, :] = first_f
    for r in range(8):
        fb[r * 128 : (r + 1) * 128, :] = jnp.broadcast_to(row[r : r + 1, :], (128, 128)).T

    WIDE = 512
    for c in range(TGT // WIDE):
        cs = slice(c * WIDE, (c + 1) * WIDE)

        def shifted(k, top):
            at = pl.ds(pl.multiple_of(k * 64, 64), 64)
            f = fb[at, :]
            value = t[at, cs] + jnp.concatenate([f] * (WIDE // 128), axis=1)
            t[at, cs] = value
            return jnp.maximum(top, fold_rows(value, jnp.maximum))

        top = lax.fori_loop(0, 16, shifted, jnp.full((8, WIDE), NEG, F32), unroll=2)
        top = jnp.max(top, axis=0, keepdims=True)

        def powers(k, total):
            at = pl.ds(pl.multiple_of(k * 64, 64), 64)
            e = jnp.exp2(t[at, cs] - top)
            t[at, cs] = e
            high, low = split2(e)
            ehi[at, cs] = high
            elo[at, cs] = low
            return total + fold_rows(e, jnp.add)

        total = lax.fori_loop(0, 16, powers, jnp.zeros((8, WIDE), F32), unroll=2)
        total = jnp.sum(total, axis=0, keepdims=True)
        logs = top + jnp.log(total) * LOG2E
        for r in range(WIDE // 128):
            at = c * (WIDE // 128) + r
            g1_out[at : at + 1, :] = logs[:, r * 128 : (r + 1) * 128]
            row[8 + at : 9 + at, :] = top[:, r * 128 : (r + 1) * 128]
        if c == 1:
            push_xy(g1_out.at[0:8], g1a_in, 3)
    push_xy(g1_out.at[8:16], g1b_in, 4)
    b = b_ref[...]
    log_b = jnp.log(b) * LOG2E

    def log_sum(slots):
        highest = jnp.max(slots[...], axis=0)
        return highest + jnp.log(jnp.sum(jnp.exp2(slots[...] - highest[None]), axis=0)) * LOG2E

    g1a_in[0] = g1_out[0:8, :]
    await_bytes(g1a_in.at[pl.ds(1, 31)], recv.at[3])
    low_logs = log_sum(g1a_in)
    g1b_in[0] = g1_out[8:16, :]
    await_bytes(g1b_in.at[pl.ds(1, 31)], recv.at[4])
    first_g = log_b - jnp.concatenate([low_logs, log_sum(g1b_in)], axis=0)
    row[8:24, :] = jnp.exp2(row[8:24, :] + first_g)
    scale = to_row(row.at[8:24, :], 16)

    def weighted(k, _):
        at = pl.ds(pl.multiple_of(k * 64, 64), 64)
        total = t[at, 0:128] * scale[:, 0:128]
        for g in range(1, GROUPS):
            gs = slice(g * 128, (g + 1) * 128)
            total += t[at, gs] * scale[:, gs]
        part[at, :] = total
        return 0

    lax.fori_loop(0, 16, weighted, 0, unroll=2)
    for r in range(8):
        f2_out[r : r + 1, :] = jnp.sum(part[r * 128 : (r + 1) * 128, :].T, axis=0, keepdims=True)
    push_zc(f2_out, f2_in, 5)
    f2_in[0] = f2_out[...]
    nx = jnp.sum(x * x, axis=0, keepdims=True) * (2.0 * LOG2E)
    from_row(row.at[24:32, :], nx, 8)
    await_bytes(f2_in.at[pl.ds(1, 15)], recv.at[5])
    sums = jnp.sum(f2_in[...], axis=0)
    ratio = a_ref[...] / sums
    row[32:40, :] = ratio
    u = to_row(row.at[32:40, :], 8)

    def stacked(points, weights):
        high, low = split2(points * weights)
        wh, wl = split2(weights)
        tail = lax.broadcasted_iota(jnp.int32, (16, weights.shape[1]), 0)
        pair = jnp.where(tail == 0, wh.astype(F32), jnp.where(tail == 1, wl.astype(F32), 0.0))
        return jnp.concatenate([high, low, pair.astype(BF16)], axis=0)

    xu = stacked(x, u)
    for half in range(2):
        sums_ref = (na, nb)[half]
        for q in range(NX):
            cs = slice(q * 512 + half * 256, q * 512 + half * 256 + 256)
            one = jnp.dot(xu, ehi[:, cs], preferred_element_type=F32)
            two = jnp.dot(xu, elo[:, cs], preferred_element_type=F32)
            w = scale[:, cs]
            sums_ref[:, q * 256 : (q + 1) * 256] = (one[0:64] + one[64:128] + two[0:64]) * w
            mass = (one[128:129] + one[129:130] + two[128:129]) * w
            at = half * 8 + q * 2
            g2_out[at : at + 1, :] = mass[:, 0:128]
            g2_out[at + 1 : at + 2, :] = mass[:, 128:256]
        if half == 0:
            push_xy(g2_out.at[0:8], g2a_in, 6)
            for dx in X_OFFSETS:
                at = pl.multiple_of(lax.rem(mx + dx, NX) * 256, 256)
                push(na.at[:, pl.ds(at, 256)], ax_in.at[dx], 7, xy(0, dx))
        else:
            push_xy(g2_out.at[8:16], g2b_in, 8)
            for dy in Y_OFFSETS:
                at = pl.multiple_of(lax.rem(my + dy, NY) * 8, 8)
                push(nb.at[pl.ds(at, 8), :], by_in.at[dy], 9, xy(dy, 0))

    own_rows = pl.ds(pl.multiple_of(my * 8, 8), 8)
    own_cols = pl.ds(pl.multiple_of(mx * 256, 256), 256)
    await_bytes(ax_in.at[pl.ds(1, 3)], recv.at[7])
    ra[...] = na[:, own_cols] + ax_in[1] + ax_in[2] + ax_in[3]
    for dy in Y_OFFSETS:
        at = pl.multiple_of(lax.rem(my + dy, NY) * 8, 8)
        push(ra.at[pl.ds(at, 8), :], ay_in.at[dy], 10, xy(dy, 0))
    await_bytes(by_in.at[pl.ds(1, 7)], recv.at[9])
    total = nb[own_rows, :]
    for k in range(1, NY):
        total += by_in[k]
    rb[...] = total
    for dx in X_OFFSETS:
        at = pl.multiple_of(lax.rem(mx + dx, NX) * 256, 256)
        push(rb.at[:, pl.ds(at, 256)], bx_in.at[dx], 11, xy(0, dx))

    g2a_in[0] = g2_out[0:8, :]
    g2b_in[0] = g2_out[8:16, :]
    await_bytes(g2a_in.at[pl.ds(1, 31)], recv.at[6])
    row[40:48, :] = jnp.sum(g2a_in[...], axis=0)
    await_bytes(g2b_in.at[pl.ds(1, 31)], recv.at[8])
    row[48:56, :] = jnp.sum(g2b_in[...], axis=0)
    for q in range(NX):
        row[56 + q * 4 : 58 + q * 4, :] = row[40 + q * 2 : 42 + q * 2, :]
        row[58 + q * 4 : 60 + q * 4, :] = row[48 + q * 2 : 50 + q * 2, :]
    ratio_g = b / row[56:72, :]
    row[72:88, :] = row[8:24, :] * ratio_g
    weights = to_row(row.at[72:88, :], 16)

    yq = stacked(y, weights)
    nt = (((1,), (1,)), ((), ()))
    for c in range(4):
        rs = slice(c * 256, (c + 1) * 256)
        one = lax.dot_general(yq, ehi[rs, :], nt, preferred_element_type=F32)
        two = lax.dot_general(yq, elo[rs, :], nt, preferred_element_type=F32)
        sn[0, :, rs] = one[0:32] + one[64:96] + two[0:32]
        sn[1, :, rs] = one[32:64] + one[96:128] + two[32:64]
        weight = one[128:129] + one[129:130] + two[128:129]
        sn[2, :, rs] = jnp.broadcast_to(weight, (32, 256))
    partner = zc(0, 1)
    push(sn.at[1 - mc], sc_in.at[pl.ds(0, 32)], 12, partner)
    push(sn.at[2, pl.ds(0, 8)], sc_in.at[pl.ds(32, 8)], 12, partner)

    def mass_of(first):
        return jnp.concatenate([row[pl.ds(first + mx * 2, 1), :], row[pl.ds(first + mx * 2 + 1, 1), :]], axis=1)

    await_bytes(ay_in.at[pl.ds(1, 7)], recv.at[10])
    total = ra[own_rows, :]
    for k in range(1, NY):
        total += ay_in[k]
    fin_t[0] = total / mass_of(40)
    for dy in Y_OFFSETS:
        push(fin_t.at[0], ta_ref.at[own_rows, own_cols], 13, xy(dy, 0))
    await_bytes(bx_in.at[pl.ds(1, 3)], recv.at[11])
    fin_t[1] = (rb[:, own_cols] + bx_in[1] + bx_in[2] + bx_in[3]) / mass_of(48)
    for dx in X_OFFSETS:
        push(fin_t.at[1], tb_ref.at[own_rows, own_cols], 14, xy(0, dx))
    ta_ref[own_rows, own_cols] = fin_t[0]
    tb_ref[own_rows, own_cols] = fin_t[1]

    await_bytes(sc_in, recv.at[12])
    for k in range(NZ):
        ks = slice(k * 128, (k + 1) * 128)
        zs[k, 0:32, :] = sn[mc, :, ks] + sc_in[0:32, ks]
        zs[k, 32:40, :] = sn[2, 0:8, ks] + sc_in[32:40, ks]
    for dz in Z_OFFSETS:
        push(zs.at[lax.rem(mz + dz, NZ)], z_in.at[dz], 15, zc(dz, 0))

    await_bytes(bx_in.at[pl.ds(1, 3)], recv.at[14])
    for dy in Y_OFFSETS:
        push(tb_ref.at[own_rows, :], tb_ref.at[own_rows, :], 16, xy(dy, 0))
    await_bytes(ay_in.at[pl.ds(1, 7)], recv.at[13])
    for dx in X_OFFSETS:
        push(ta_ref.at[:, own_cols], ta_ref.at[:, own_cols], 17, xy(0, dx))

    sa_in[0] = sa_out[...]
    sb_in[0] = sb_out[...]
    await_bytes(sa_in.at[pl.ds(1, 31)], recv.at[1])
    await_bytes(sb_in.at[pl.ds(1, 15)], recv.at[2])
    log_sa = jnp.log(jnp.sum(sa_in[...], axis=0))
    log_sb = jnp.log(jnp.sum(sb_in[...], axis=0))
    fg_ref[0:8, :] = (0.5 * LN2) * (first_f + row[24:32, :]) + 0.5 * jnp.log(ratio) - (log_sa - 0.5 * log_sb)
    fg_ref[8:24, :] = (0.5 * LN2) * first_g + 0.5 * jnp.log(ratio_g) - (log_sb - log_sa)
    stores = [fetch(fg_ref, fg_hbm, 4)]

    await_bytes(z_in.at[pl.ds(1, 7)], recv.at[15])
    total = zs[mz]
    for k in range(1, NZ):
        total += z_in[k]
    fin[...] = total[0:32] / total[32:33]
    push(fin, fin_in, 18, partner)
    await_bytes(fin_in, recv.at[18])
    mine, other = fin[...], fin_in[...]
    low = jnp.where(mc == 0, mine, other)
    high = jnp.where(mc == 0, other, mine)
    both = jnp.concatenate([low, high], axis=0)
    smap_ref[...] = jnp.where(mc == 0, both[:, 0:64], both[:, 64:128])
    stores.append(fetch(smap_ref, smap_hbm, 5))

    await_bytes(ax_in.at[pl.ds(1, 3)], recv.at[17])
    for q in range(NX):
        stores.append(fetch(ta_ref.at[:, q * 256 : q * 256 + 256], tmap_hbm.at[:, q * 512 : q * 512 + 256], 6 + q))
    await_bytes(by_in.at[pl.ds(1, 7)], recv.at[16])
    for q in range(NX):
        stores.append(fetch(tb_ref.at[:, q * 256 : q * 256 + 256], tmap_hbm.at[:, q * 512 + 256 : q * 512 + 512], 10 + q))

    await_bytes(f1_in.at[pl.ds(1, 15)], send.at[0])
    await_bytes(sa_in.at[pl.ds(1, 31)], send.at[1])
    await_bytes(sb_in.at[pl.ds(1, 15)], send.at[2])
    await_bytes(g1a_in.at[pl.ds(1, 31)], send.at[3])
    await_bytes(g1b_in.at[pl.ds(1, 31)], send.at[4])
    await_bytes(f2_in.at[pl.ds(1, 15)], send.at[5])
    await_bytes(g2a_in.at[pl.ds(1, 31)], send.at[6])
    await_bytes(ax_in.at[pl.ds(1, 3)], send.at[7])
    await_bytes(g2b_in.at[pl.ds(1, 31)], send.at[8])
    await_bytes(by_in.at[pl.ds(1, 7)], send.at[9])
    await_bytes(ay_in.at[pl.ds(1, 7)], send.at[10])
    await_bytes(bx_in.at[pl.ds(1, 3)], send.at[11])
    await_bytes(sc_in, send.at[12])
    await_bytes(ay_in.at[pl.ds(1, 7)], send.at[13])
    await_bytes(bx_in.at[pl.ds(1, 3)], send.at[14])
    await_bytes(z_in.at[pl.ds(1, 7)], send.at[15])
    await_bytes(by_in.at[pl.ds(1, 7)], send.at[16])
    await_bytes(ax_in.at[pl.ds(1, 3)], send.at[17])
    await_bytes(fin_in, send.at[18])
    for copy in stores:
        copy.wait()


def finish(fg, sm, tm, f_hbm, g_hbm, smap_hbm, tmap_hbm, fg_v, sm_v, tm_v, come, go):
    loads = [pltpu.make_async_copy(tm.at[k * 32 : k * 32 + 32], tm_v.at[k * 32 : k * 32 + 32], come.at[k]) for k in range(2)]
    loads += [pltpu.make_async_copy(sm, sm_v, come.at[2]), pltpu.make_async_copy(fg, fg_v, come.at[3])]
    stores = [pltpu.make_async_copy(tm_v.at[k * 32 : k * 32 + 32], tmap_hbm.at[k * 32 : k * 32 + 32], go.at[k]) for k in range(2)]
    stores += [
        pltpu.make_async_copy(sm_v, smap_hbm, go.at[2]),
        pltpu.make_async_copy(fg_v.at[0:8], f_hbm, go.at[3]),
        pltpu.make_async_copy(fg_v.at[8:24], g_hbm, go.at[4]),
    ]
    for copy in loads:
        copy.start()
    for k, copy in enumerate(loads):
        copy.wait()
        stores[k].start()
    stores[4].start()
    for copy in stores:
        copy.wait()


def local(source_cells, target_cells, source_mass, target_mass):
    anywhere = pl.BlockSpec(memory_space=pl.ANY)
    results = pl.pallas_call(
        kernel,
        out_shape=(
            jax.ShapeDtypeStruct((24, 128), F32),
            jax.ShapeDtypeStruct((DIMS, 64), F32),
            jax.ShapeDtypeStruct((DIMS, TGT), F32),
        ),
        in_specs=[anywhere] * 4,
        out_specs=(anywhere,) * 3,
        scratch_shapes=[
            pltpu.VMEM((DIMS, SRC), F32),
            pltpu.VMEM((DIMS, TGT), F32),
            pltpu.VMEM((8, 128), F32),
            pltpu.VMEM((16, 128), F32),
            pltpu.VMEM((24, 128), F32),
            pltpu.VMEM((DIMS, 64), F32),
            pltpu.VMEM((DIMS, SRC), F32),
            pltpu.VMEM((DIMS, SRC), F32),
            pltpu.VMEM((SRC, 512), BF16),
            pltpu.VMEM((512, TGT), BF16),
            pltpu.VMEM((SRC, TGT), F32),
            pltpu.VMEM((SRC, TGT), BF16),
            pltpu.VMEM((SRC, TGT), BF16),
            pltpu.VMEM((SRC, 128), F32),
            pltpu.VMEM((SRC, 128), F32),
            pltpu.VMEM((8, 128), F32),
            pltpu.VMEM((16, 8, 128), F32),
            pltpu.VMEM((8, 128), F32),
            pltpu.VMEM((16, 8, 128), F32),
            pltpu.VMEM((16, 128), F32),
            pltpu.VMEM((32, 8, 128), F32),
            pltpu.VMEM((32, 8, 128), F32),
            pltpu.VMEM((16, 128), F32),
            pltpu.VMEM((32, 8, 128), F32),
            pltpu.VMEM((32, 8, 128), F32),
            pltpu.VMEM((1, 128), F32),
            pltpu.VMEM((32, 1, 128), F32),
            pltpu.VMEM((1, 128), F32),
            pltpu.VMEM((16, 1, 128), F32),
            pltpu.VMEM((88, 128), F32),
            pltpu.VMEM((DIMS, SRC), F32),
            pltpu.VMEM((DIMS, SRC), F32),
            pltpu.VMEM((NX, DIMS, 256), F32),
            pltpu.VMEM((DIMS, 256), F32),
            pltpu.VMEM((NY, 8, 256), F32),
            pltpu.VMEM((NY, 8, SRC), F32),
            pltpu.VMEM((8, SRC), F32),
            pltpu.VMEM((NX, 8, 256), F32),
            pltpu.VMEM((2, 8, 256), F32),
            pltpu.VMEM((3, 32, SRC), F32),
            pltpu.VMEM((40, SRC), F32),
            pltpu.VMEM((NZ, 40, 128), F32),
            pltpu.VMEM((NZ, 40, 128), F32),
            pltpu.VMEM((32, 128), F32),
            pltpu.VMEM((32, 128), F32),
            pltpu.SemaphoreType.DMA((19,)),
            pltpu.SemaphoreType.DMA((19,)),
            pltpu.SemaphoreType.DMA((14,)),
        ],
        compiler_params=pltpu.CompilerParams(
            collective_id=0, has_side_effects=True, vmem_limit_bytes=60 << 20
        ),
    )(source_cells, target_cells, source_mass.reshape(8, 128), target_mass.reshape(16, 128))
    f, g, smap, tmap = pl.pallas_call(
        finish,
        out_shape=(
            jax.ShapeDtypeStruct((8, 128), F32),
            jax.ShapeDtypeStruct((16, 128), F32),
            jax.ShapeDtypeStruct((DIMS, 64), F32),
            jax.ShapeDtypeStruct((DIMS, TGT), F32),
        ),
        in_specs=[anywhere] * 3,
        out_specs=(anywhere,) * 4,
        scratch_shapes=[
            pltpu.VMEM((24, 128), F32),
            pltpu.VMEM((DIMS, 64), F32),
            pltpu.VMEM((DIMS, TGT), F32),
            pltpu.SemaphoreType.DMA((4,)),
            pltpu.SemaphoreType.DMA((5,)),
        ],
    )(*results)
    return f.reshape(-1), g.reshape(-1), smap, tmap


def solution(mesh):
    in_specs = (P(None, "rows"), P(None, "cols"), P("rows"), P("cols"))
    out_specs = (P("rows"), P("cols"), P(None, ("rows", "cols")), P(None, "cols"))
    return jax.shard_map(local, mesh=mesh, in_specs=in_specs, out_specs=out_specs, check_vma=False)
```

time: 79 us -> 68.5 us (0.87)
  Pallas kernels: 73 us -> 67.7 us
  local copies, waits for them, and re-layouts: 5.06 us -> 0 us
    pallas_call x1 -> x2, Pallas kernels: 73 us -> 67.7 us  [the longest x1 65.9 us: local(): pl.pallas_call(kernel, out_shape=(jax.ShapeDtypeStruct((24, 128), F32), j...]
    unnamed x6 -> x0, local copies, waits for them, and re-layouts: 5.06 us -> none
where the time goes in v2:
time: 68.5 us; the launch traced here: 68.4 us
  Pallas kernels  67.7 us (99%)
    pallas_call x1, Pallas kernels, local(): pl.pallas_call(kernel, out_shape=(jax.ShapeDtypeStruct((24, 128), F32), j...  65.9 us
    pallas_call x1, Pallas kernels, local(): pl.pallas_call(finish, out_shape=(jax.ShapeDtypeStruct((8, 128), F32), ja...  1.82 us

profile of v2, /device:TPU:1, one launch (start us, length us, event | category | flops | bytes accessed | tf_op | source)
XLA Modules:
  0.0 68.4 jit_solution(4001534583431676144)
XLA Ops:
  0.6 65.9 %shard_map.75 = (f32[24,128]{1,0:T(8,128)}, f32[64,64]{1,0:T(8,128)}, f32[64,2048]{1,0:T(8,128)}) custom-call(f32[64,1024]{1,0:T(8,128)} %x_hbm.1, f32[64,2048]{1,0:T(8,128)} %y_hbm.1, f32[8,128]{1,0:T(8,128)} %bitcast.5, f32[16,128]{1,0:T(8,128)} %bitcast.4), custom_call_target="tpu_custom_call" | custom-call | tf_op jit(solution)/shard_map/pallas_call | solution.py:447
  66.5 1.8 %shard_map.76 = (f32[8,128]{1,0:T(8,128)}, f32[16,128]{1,0:T(8,128)}, f32[64,64]{1,0:T(8,128)}, f32[64,2048]{1,0:T(8,128)}) custom-call(f32[24,128]{1,0:T(8,128)} %get-tuple-element.11.fg, f32[64,64]{1,0:T(8,128)} %get-tuple-element.12.sm, f32[64,2048]{1,0:T(8,128)} %get-tuple-element.13.tm), custom_call_target="tpu_custom_call" | custom-call | tf_op jit(solution)/shard_map/pallas_call | solution.py:510

commit v3 on v2

--- a/solution.py
+++ b/solution.py
@@ -72,11 +72,11 @@
 def kernel(
     x_hbm, y_hbm, a_hbm, b_hbm,
     fg_hbm, smap_hbm, tmap_hbm,
-    x_ref, y_ref, a_ref, b_ref, fg_ref, smap_ref, ta_ref, tb_ref,
+    x_ref, y_ref, a_ref, b_ref, fg_ref, smap_ref, tmap_ref,
     xt, yk, t, ehi, elo, fb, part,
-    f1_out, f1_in, f2_out, f2_in, g1_out, g1a_in, g1b_in, g2_out, g2a_in, g2b_in,
+    f1_out, f1_in, f2_out, f2_in, g1_out, g1a_in, g1b_in, g2_out, g2y_in, g2_mid, g2x_in,
     sa_out, sa_in, sb_out, sb_in, row,
-    na, nb, ax_in, ra, ay_in, by_in, rb, bx_in, fin_t,
+    tn, ax_in, ra, ay_in, by_in, rb, bx_in, fin_t,
     sn, sc_in, zs, z_in, fin, fin_in,
     send, recv, near,
 ):
@@ -270,104 +270,142 @@
         pair = jnp.where(tail == 0, wh.astype(F32), jnp.where(tail == 1, wl.astype(F32), 0.0))
         return jnp.concatenate([high, low, pair.astype(BF16)], axis=0)
 
+    def rows_of(dy):
+        return pl.ds(pl.multiple_of(lax.rem(my + dy, NY) * 8, 8), 8)
+
+    def cols_of(dx):
+        return pl.ds(pl.multiple_of(lax.rem(mx + dx, NX) * 128, 128), 128)
+
+    own_rows, own_cols = rows_of(0), cols_of(0)
+
+    def gather_x(p):
+        for dx in X_OFFSETS:
+            push(tn.at[p, :, cols_of(dx)], ax_in.at[p, dx], 23 + p, xy(0, dx))
+
+    def scatter_y(p):
+        await_bytes(ax_in.at[p, pl.ds(1, 3)], recv.at[23 + p])
+        ra[p] = tn[p, :, own_cols] + ax_in[p, 1] + ax_in[p, 2] + ax_in[p, 3]
+        for dy in Y_OFFSETS:
+            push(ra.at[p, rows_of(dy), :], ay_in.at[p, dy], 26 + p, xy(dy, 0))
+
+    def return_y(p):
+        await_bytes(ay_in.at[p, pl.ds(1, 7)], recv.at[26 + p])
+        total = ra[p, own_rows, :]
+        for k in range(1, NY):
+            total += ay_in[p, k]
+        fin_t[p] = total / row[pl.ds(56 + mx * 4 + p, 1), :]
+        for dy in Y_OFFSETS:
+            push(fin_t.at[p], tmap_ref.at[p, own_rows, own_cols], 29 + p, xy(dy, 0))
+        tmap_ref[p, own_rows, own_cols] = fin_t[p]
+
+    def return_x(p):
+        await_bytes(ay_in.at[p, pl.ds(1, 7)], recv.at[29 + p])
+        for dx in X_OFFSETS:
+            push(tmap_ref.at[p, :, own_cols], tmap_ref.at[p, :, own_cols], 32 + p, xy(0, dx))
+
     xu = stacked(x, u)
     for half in range(2):
-        sums_ref = (na, nb)[half]
         for q in range(NX):
             cs = slice(q * 512 + half * 256, q * 512 + half * 256 + 256)
             one = jnp.dot(xu, ehi[:, cs], preferred_element_type=F32)
             two = jnp.dot(xu, elo[:, cs], preferred_element_type=F32)
             w = scale[:, cs]
-            sums_ref[:, q * 256 : (q + 1) * 256] = (one[0:64] + one[64:128] + two[0:64]) * w
+            sums = (one[0:64] + one[64:128] + two[0:64]) * w
+            tn[half * 2, :, q * 128 : (q + 1) * 128] = sums[:, 0:128]
+            tn[half * 2 + 1, :, q * 128 : (q + 1) * 128] = sums[:, 128:256]
             mass = (one[128:129] + one[129:130] + two[128:129]) * w
-            at = half * 8 + q * 2
+            at = q * 4 + half * 2
             g2_out[at : at + 1, :] = mass[:, 0:128]
             g2_out[at + 1 : at + 2, :] = mass[:, 128:256]
         if half == 0:
-            push_xy(g2_out.at[0:8], g2a_in, 6)
-            for dx in X_OFFSETS:
-                at = pl.multiple_of(lax.rem(mx + dx, NX) * 256, 256)
-                push(na.at[:, pl.ds(at, 256)], ax_in.at[dx], 7, xy(0, dx))
-        else:
-            push_xy(g2_out.at[8:16], g2b_in, 8)
-            for dy in Y_OFFSETS:
-                at = pl.multiple_of(lax.rem(my + dy, NY) * 8, 8)
-                push(nb.at[pl.ds(at, 8), :], by_in.at[dy], 9, xy(dy, 0))
-
-    own_rows = pl.ds(pl.multiple_of(my * 8, 8), 8)
-    own_cols = pl.ds(pl.multiple_of(mx * 256, 256), 256)
-    await_bytes(ax_in.at[pl.ds(1, 3)], recv.at[7])
-    ra[...] = na[:, own_cols] + ax_in[1] + ax_in[2] + ax_in[3]
+            gather_x(0)
+            gather_x(1)
     for dy in Y_OFFSETS:
-        at = pl.multiple_of(lax.rem(my + dy, NY) * 8, 8)
-        push(ra.at[pl.ds(at, 8), :], ay_in.at[dy], 10, xy(dy, 0))
+        push(g2_out, g2y_in.at[dy], 6, xy(dy, 0))
+    for dy in Y_OFFSETS:
+        push(tn.at[3, rows_of(dy), :], by_in.at[dy], 9, xy(dy, 0))
+    gather_x(2)
+
+    scatter_y(0)
+    scatter_y(1)
+    g2y_in[0] = g2_out[...]
+    await_bytes(g2y_in.at[pl.ds(1, 7)], recv.at[6])
+    g2_mid[...] = jnp.sum(g2y_in[...], axis=0)
+    for dx in X_OFFSETS:
+        push(g2_mid, g2x_in.at[dx], 8, xy(0, dx))
+    scatter_y(2)
     await_bytes(by_in.at[pl.ds(1, 7)], recv.at[9])
-    total = nb[own_rows, :]
+    total = tn[3, own_rows, :]
     for k in range(1, NY):
         total += by_in[k]
     rb[...] = total
     for dx in X_OFFSETS:
-        at = pl.multiple_of(lax.rem(mx + dx, NX) * 256, 256)
-        push(rb.at[:, pl.ds(at, 256)], bx_in.at[dx], 11, xy(0, dx))
-
-    g2a_in[0] = g2_out[0:8, :]
-    g2b_in[0] = g2_out[8:16, :]
-    await_bytes(g2a_in.at[pl.ds(1, 31)], recv.at[6])
-    row[40:48, :] = jnp.sum(g2a_in[...], axis=0)
-    await_bytes(g2b_in.at[pl.ds(1, 31)], recv.at[8])
-    row[48:56, :] = jnp.sum(g2b_in[...], axis=0)
-    for q in range(NX):
-        row[56 + q * 4 : 58 + q * 4, :] = row[40 + q * 2 : 42 + q * 2, :]
-        row[58 + q * 4 : 60 + q * 4, :] = row[48 + q * 2 : 50 + q * 2, :]
+        push(rb.at[:, cols_of(dx)], bx_in.at[dx], 11, xy(0, dx))
+
+    g2x_in[0] = g2_mid[...]
+    await_bytes(g2x_in.at[pl.ds(1, 3)], recv.at[8])
+    row[56:72, :] = jnp.sum(g2x_in[...], axis=0)
     ratio_g = b / row[56:72, :]
     row[72:88, :] = row[8:24, :] * ratio_g
     weights = to_row(row.at[72:88, :], 16)
 
     yq = stacked(y, weights)
     nt = (((1,), (1,)), ((), ()))
-    for c in range(4):
-        rs = slice(c * 256, (c + 1) * 256)
+    partner = zc(0, 1)
+    own_pair = mz // 2
+    pairs = [lax.rem(own_pair + k, NZ // 2) for k in (2, 1, 3, 0)]
+
+    def chunk(k):
+        rs = pl.ds(pl.multiple_of(pairs[k] * 256, 256), 256)
         one = lax.dot_general(yq, ehi[rs, :], nt, preferred_element_type=F32)
         two = lax.dot_general(yq, elo[rs, :], nt, preferred_element_type=F32)
-        sn[0, :, rs] = one[0:32] + one[64:96] + two[0:32]
-        sn[1, :, rs] = one[32:64] + one[96:128] + two[32:64]
+        sn[k, 0:64, :] = one[0:64] + one[64:128] + two[0:64]
         weight = one[128:129] + one[129:130] + two[128:129]
-        sn[2, :, rs] = jnp.broadcast_to(weight, (32, 256))
-    partner = zc(0, 1)
-    push(sn.at[1 - mc], sc_in.at[pl.ds(0, 32)], 12, partner)
-    push(sn.at[2, pl.ds(0, 8)], sc_in.at[pl.ds(32, 8)], 12, partner)
-
-    def mass_of(first):
-        return jnp.concatenate([row[pl.ds(first + mx * 2, 1), :], row[pl.ds(first + mx * 2 + 1, 1), :]], axis=1)
-
-    await_bytes(ay_in.at[pl.ds(1, 7)], recv.at[10])
-    total = ra[own_rows, :]
-    for k in range(1, NY):
-        total += ay_in[k]
-    fin_t[0] = total / mass_of(40)
-    for dy in Y_OFFSETS:
-        push(fin_t.at[0], ta_ref.at[own_rows, own_cols], 13, xy(dy, 0))
+        sn[k, 64:72, :] = jnp.broadcast_to(weight, (8, 256))
+        theirs = pl.ds(pl.multiple_of((1 - mc) * 32, 32), 32)
+        push(sn.at[k, theirs], sc_in.at[k, pl.ds(0, 32)], 19 + k, partner)
+        push(sn.at[k, pl.ds(64, 8)], sc_in.at[k, pl.ds(32, 8)], 19 + k, partner)
+
+    def onward(k):
+        await_bytes(sc_in.at[k], recv.at[19 + k])
+        mine = pl.ds(pl.multiple_of(mc * 32, 32), 32)
+        for e in range(2):
+            es = slice(e * 128, (e + 1) * 128)
+            zs[k * 2 + e, 0:32, :] = sn[k, mine, es] + sc_in[k, 0:32, es]
+            zs[k * 2 + e, 32:40, :] = sn[k, 64:72, es] + sc_in[k, 32:40, es]
+        if k < 3:
+            for e in range(2):
+                to = pairs[k] * 2 + e
+                hops = lax.rem(to - mz + NZ, NZ)
+                push(zs.at[k * 2 + e], z_in.at[hops], 15, (rows_at, to * NC + mc))
+        else:
+            to = own_pair * 2 + 1 - lax.rem(mz, 2)
+            hops = lax.rem(to - mz + NZ, NZ)
+            push(zs.at[6 + 1 - lax.rem(mz, 2)], z_in.at[hops], 15, (rows_at, to * NC + mc))
+
+    chunk(0)
+    return_y(0)
+    return_y(1)
     await_bytes(bx_in.at[pl.ds(1, 3)], recv.at[11])
-    fin_t[1] = (rb[:, own_cols] + bx_in[1] + bx_in[2] + bx_in[3]) / mass_of(48)
+    fin_t[3] = (rb[:, own_cols] + bx_in[1] + bx_in[2] + bx_in[3]) / row[pl.ds(56 + mx * 4 + 3, 1), :]
     for dx in X_OFFSETS:
-        push(fin_t.at[1], tb_ref.at[own_rows, own_cols], 14, xy(0, dx))
-    ta_ref[own_rows, own_cols] = fin_t[0]
-    tb_ref[own_rows, own_cols] = fin_t[1]
-
-    await_bytes(sc_in, recv.at[12])
-    for k in range(NZ):
-        ks = slice(k * 128, (k + 1) * 128)
-        zs[k, 0:32, :] = sn[mc, :, ks] + sc_in[0:32, ks]
-        zs[k, 32:40, :] = sn[2, 0:8, ks] + sc_in[32:40, ks]
-    for dz in Z_OFFSETS:
-        push(zs.at[lax.rem(mz + dz, NZ)], z_in.at[dz], 15, zc(dz, 0))
-
+        push(fin_t.at[3], tmap_ref.at[3, own_rows, own_cols], 14, xy(0, dx))
+    tmap_ref[3, own_rows, own_cols] = fin_t[3]
+    chunk(1)
+    onward(0)
+    return_y(2)
+    chunk(2)
+    onward(1)
+    chunk(3)
+    onward(2)
+    onward(3)
+
+    return_x(0)
     await_bytes(bx_in.at[pl.ds(1, 3)], recv.at[14])
     for dy in Y_OFFSETS:
-        push(tb_ref.at[own_rows, :], tb_ref.at[own_rows, :], 16, xy(dy, 0))
-    await_bytes(ay_in.at[pl.ds(1, 7)], recv.at[13])
-    for dx in X_OFFSETS:
-        push(ta_ref.at[:, own_cols], ta_ref.at[:, own_cols], 17, xy(0, dx))
+        push(tmap_ref.at[3, own_rows, :], tmap_ref.at[3, own_rows, :], 16, xy(dy, 0))
+    return_x(1)
+    return_x(2)
 
     sa_in[0] = sa_out[...]
     sb_in[0] = sb_out[...]
@@ -380,7 +418,7 @@
     stores = [fetch(fg_ref, fg_hbm, 4)]
 
     await_bytes(z_in.at[pl.ds(1, 7)], recv.at[15])
-    total = zs[mz]
+    total = zs[6 + lax.rem(mz, 2)]
     for k in range(1, NZ):
         total += z_in[k]
     fin[...] = total[0:32] / total[32:33]
@@ -393,12 +431,19 @@
     smap_ref[...] = jnp.where(mc == 0, both[:, 0:64], both[:, 64:128])
     stores.append(fetch(smap_ref, smap_hbm, 5))
 
-    await_bytes(ax_in.at[pl.ds(1, 3)], recv.at[17])
-    for q in range(NX):
-        stores.append(fetch(ta_ref.at[:, q * 256 : q * 256 + 256], tmap_hbm.at[:, q * 512 : q * 512 + 256], 6 + q))
+    def store(p):
+        for q in range(NX):
+            place = tmap_hbm.at[:, q * 512 + p * 128 : q * 512 + p * 128 + 128]
+            stores.append(fetch(tmap_ref.at[p, :, q * 128 : q * 128 + 128], place, 6 + p * 4 + q))
+
+    await_bytes(ax_in.at[0, pl.ds(1, 3)], recv.at[32])
+    store(0)
+    await_bytes(ax_in.at[1, pl.ds(1, 3)], recv.at[33])
+    store(1)
     await_bytes(by_in.at[pl.ds(1, 7)], recv.at[16])
-    for q in range(NX):
-        stores.append(fetch(tb_ref.at[:, q * 256 : q * 256 + 256], tmap_hbm.at[:, q * 512 + 256 : q * 512 + 512], 10 + q))
+    store(3)
+    await_bytes(ax_in.at[2, pl.ds(1, 3)], recv.at[34])
+    store(2)
 
     await_bytes(f1_in.at[pl.ds(1, 15)], send.at[0])
     await_bytes(sa_in.at[pl.ds(1, 31)], send.at[1])
@@ -406,18 +451,20 @@
     await_bytes(g1a_in.at[pl.ds(1, 31)], send.at[3])
     await_bytes(g1b_in.at[pl.ds(1, 31)], send.at[4])
     await_bytes(f2_in.at[pl.ds(1, 15)], send.at[5])
-    await_bytes(g2a_in.at[pl.ds(1, 31)], send.at[6])
-    await_bytes(ax_in.at[pl.ds(1, 3)], send.at[7])
-    await_bytes(g2b_in.at[pl.ds(1, 31)], send.at[8])
+    await_bytes(g2y_in.at[pl.ds(1, 7)], send.at[6])
+    await_bytes(g2x_in.at[pl.ds(1, 3)], send.at[8])
     await_bytes(by_in.at[pl.ds(1, 7)], send.at[9])
-    await_bytes(ay_in.at[pl.ds(1, 7)], send.at[10])
     await_bytes(bx_in.at[pl.ds(1, 3)], send.at[11])
-    await_bytes(sc_in, send.at[12])
-    await_bytes(ay_in.at[pl.ds(1, 7)], send.at[13])
+    for k in range(4):
+        await_bytes(sc_in.at[k], send.at[19 + k])
     await_bytes(bx_in.at[pl.ds(1, 3)], send.at[14])
     await_bytes(z_in.at[pl.ds(1, 7)], send.at[15])
     await_bytes(by_in.at[pl.ds(1, 7)], send.at[16])
-    await_bytes(ax_in.at[pl.ds(1, 3)], send.at[17])
+    for p in range(3):
+        await_bytes(ax_in.at[p, pl.ds(1, 3)], send.at[23 + p])
+        await_bytes(ay_in.at[p, pl.ds(1, 7)], send.at[26 + p])
+        await_bytes(ay_in.at[p, pl.ds(1, 7)], send.at[29 + p])
+        await_bytes(ax_in.at[p, pl.ds(1, 3)], send.at[32 + p])
     await_bytes(fin_in, send.at[18])
     for copy in stores:
         copy.wait()
@@ -460,8 +507,7 @@
             pltpu.VMEM((16, 128), F32),
             pltpu.VMEM((24, 128), F32),
             pltpu.VMEM((DIMS, 64), F32),
-            pltpu.VMEM((DIMS, SRC), F32),
-            pltpu.VMEM((DIMS, SRC), F32),
+            pltpu.VMEM((4, DIMS, 512), F32),
             pltpu.VMEM((SRC, 512), BF16),
             pltpu.VMEM((512, TGT), BF16),
             pltpu.VMEM((SRC, TGT), F32),
@@ -477,31 +523,31 @@
             pltpu.VMEM((32, 8, 128), F32),
             pltpu.VMEM((32, 8, 128), F32),
             pltpu.VMEM((16, 128), F32),
-            pltpu.VMEM((32, 8, 128), F32),
-            pltpu.VMEM((32, 8, 128), F32),
+            pltpu.VMEM((NY, 16, 128), F32),
+            pltpu.VMEM((16, 128), F32),
+            pltpu.VMEM((NX, 16, 128), F32),
             pltpu.VMEM((1, 128), F32),
             pltpu.VMEM((32, 1, 128), F32),
             pltpu.VMEM((1, 128), F32),
             pltpu.VMEM((16, 1, 128), F32),
             pltpu.VMEM((88, 128), F32),
-            pltpu.VMEM((DIMS, SRC), F32),
-            pltpu.VMEM((DIMS, SRC), F32),
-            pltpu.VMEM((NX, DIMS, 256), F32),
-            pltpu.VMEM((DIMS, 256), F32),
-            pltpu.VMEM((NY, 8, 256), F32),
-            pltpu.VMEM((NY, 8, SRC), F32),
-            pltpu.VMEM((8, SRC), F32),
-            pltpu.VMEM((NX, 8, 256), F32),
-            pltpu.VMEM((2, 8, 256), F32),
-            pltpu.VMEM((3, 32, SRC), F32),
-            pltpu.VMEM((40, SRC), F32),
+            pltpu.VMEM((4, DIMS, 512), F32),
+            pltpu.VMEM((3, NX, DIMS, 128), F32),
+            pltpu.VMEM((3, DIMS, 128), F32),
+            pltpu.VMEM((3, NY, 8, 128), F32),
+            pltpu.VMEM((NY, 8, 512), F32),
+            pltpu.VMEM((8, 512), F32),
+            pltpu.VMEM((NX, 8, 128), F32),
+            pltpu.VMEM((4, 8, 128), F32),
+            pltpu.VMEM((4, 72, 256), F32),
+            pltpu.VMEM((4, 40, 256), F32),
             pltpu.VMEM((NZ, 40, 128), F32),
             pltpu.VMEM((NZ, 40, 128), F32),
             pltpu.VMEM((32, 128), F32),
             pltpu.VMEM((32, 128), F32),
-            pltpu.SemaphoreType.DMA((19,)),
-            pltpu.SemaphoreType.DMA((19,)),
-            pltpu.SemaphoreType.DMA((14,)),
+            pltpu.SemaphoreType.DMA((35,)),
+            pltpu.SemaphoreType.DMA((35,)),
+            pltpu.SemaphoreType.DMA((22,)),
         ],
         compiler_params=pltpu.CompilerParams(
             collective_id=0, has_side_effects=True, vmem_limit_bytes=60 << 20

time: 68.5 us -> 65.5 us (0.956)
  Pallas kernels: 67.7 us -> 64.7 us
    pallas_call x1, Pallas kernels: 65.9 us -> 62.9 us  [local(): pl.pallas_call(kernel, out_shape=(jax.ShapeDtypeStruct((24, 128), F32), j...]
where the time goes in v3:
time: 65.5 us; the launch traced here: 65.3 us
  Pallas kernels  64.7 us (99%)
    pallas_call x1, Pallas kernels, local(): pl.pallas_call(kernel, out_shape=(jax.ShapeDtypeStruct((24, 128), F32), j...  62.9 us
    pallas_call x1, Pallas kernels, local(): pl.pallas_call(finish, out_shape=(jax.ShapeDtypeStruct((8, 128), F32), ja...  1.82 us

profile of v3, /device:TPU:1, one launch (start us, length us, event | category | flops | bytes accessed | tf_op | source)
XLA Modules:
  0.0 65.3 jit_solution(10733739656887547524)
XLA Ops:
  0.6 62.9 %shard_map.75 = (f32[24,128]{1,0:T(8,128)}, f32[64,64]{1,0:T(8,128)}, f32[64,2048]{1,0:T(8,128)}) custom-call(f32[64,1024]{1,0:T(8,128)} %x_hbm.1, f32[64,2048]{1,0:T(8,128)} %y_hbm.1, f32[8,128]{1,0:T(8,128)} %bitcast.5, f32[16,128]{1,0:T(8,128)} %bitcast.4), custom_call_target="tpu_custom_call" | custom-call | tf_op jit(solution)/shard_map/pallas_call | solution.py:494
  63.5 1.8 %shard_map.76 = (f32[8,128]{1,0:T(8,128)}, f32[16,128]{1,0:T(8,128)}, f32[64,64]{1,0:T(8,128)}, f32[64,2048]{1,0:T(8,128)}) custom-call(f32[24,128]{1,0:T(8,128)} %get-tuple-element.11.fg, f32[64,64]{1,0:T(8,128)} %get-tuple-element.12.sm, f32[64,2048]{1,0:T(8,128)} %get-tuple-element.13.tm), custom_call_target="tpu_custom_call" | custom-call | tf_op jit(solution)/shard_map/pallas_call | solution.py:556

commit v4 on v3

--- a/solution.py
+++ b/solution.py
@@ -359,20 +359,20 @@
         rs = pl.ds(pl.multiple_of(pairs[k] * 256, 256), 256)
         one = lax.dot_general(yq, ehi[rs, :], nt, preferred_element_type=F32)
         two = lax.dot_general(yq, elo[rs, :], nt, preferred_element_type=F32)
-        sn[k, 0:64, :] = one[0:64] + one[64:128] + two[0:64]
-        weight = one[128:129] + one[129:130] + two[128:129]
-        sn[k, 64:72, :] = jnp.broadcast_to(weight, (8, 256))
-        theirs = pl.ds(pl.multiple_of((1 - mc) * 32, 32), 32)
-        push(sn.at[k, theirs], sc_in.at[k, pl.ds(0, 32)], 19 + k, partner)
-        push(sn.at[k, pl.ds(64, 8)], sc_in.at[k, pl.ds(32, 8)], 19 + k, partner)
+        sn[k, 0:32, :] = one[0:32] + one[64:96] + two[0:32]
+        sn[k, 40:72, :] = one[32:64] + one[96:128] + two[32:64]
+        weight = jnp.broadcast_to(one[128:129] + one[129:130] + two[128:129], (8, 256))
+        sn[k, 32:40, :] = weight
+        sn[k, 72:80, :] = weight
+        theirs = pl.ds(pl.multiple_of((1 - mc) * 40, 8), 40)
+        push(sn.at[k, theirs], sc_in.at[k], 19 + k, partner)
 
     def onward(k):
         await_bytes(sc_in.at[k], recv.at[19 + k])
-        mine = pl.ds(pl.multiple_of(mc * 32, 32), 32)
+        mine = pl.ds(pl.multiple_of(mc * 40, 8), 40)
         for e in range(2):
             es = slice(e * 128, (e + 1) * 128)
-            zs[k * 2 + e, 0:32, :] = sn[k, mine, es] + sc_in[k, 0:32, es]
-            zs[k * 2 + e, 32:40, :] = sn[k, 64:72, es] + sc_in[k, 32:40, es]
+            zs[k * 2 + e] = sn[k, mine, es] + sc_in[k, :, es]
         if k < 3:
             for e in range(2):
                 to = pairs[k] * 2 + e
@@ -384,20 +384,20 @@
             push(zs.at[6 + 1 - lax.rem(mz, 2)], z_in.at[hops], 15, (rows_at, to * NC + mc))
 
     chunk(0)
+    chunk(1)
+    onward(0)
     return_y(0)
     return_y(1)
+    chunk(2)
+    onward(1)
     await_bytes(bx_in.at[pl.ds(1, 3)], recv.at[11])
     fin_t[3] = (rb[:, own_cols] + bx_in[1] + bx_in[2] + bx_in[3]) / row[pl.ds(56 + mx * 4 + 3, 1), :]
     for dx in X_OFFSETS:
         push(fin_t.at[3], tmap_ref.at[3, own_rows, own_cols], 14, xy(0, dx))
     tmap_ref[3, own_rows, own_cols] = fin_t[3]
-    chunk(1)
-    onward(0)
-    return_y(2)
-    chunk(2)
-    onward(1)
     chunk(3)
     onward(2)
+    return_y(2)
     onward(3)
 
     return_x(0)
@@ -539,7 +539,7 @@
             pltpu.VMEM((8, 512), F32),
             pltpu.VMEM((NX, 8, 128), F32),
             pltpu.VMEM((4, 8, 128), F32),
-            pltpu.VMEM((4, 72, 256), F32),
+            pltpu.VMEM((4, 80, 256), F32),
             pltpu.VMEM((4, 40, 256), F32),
             pltpu.VMEM((NZ, 40, 128), F32),
             pltpu.VMEM((NZ, 40, 128), F32),

time: 65.5 us -> 64.1 us (0.979)
  Pallas kernels: 64.7 us -> 63.3 us
    pallas_call x1, Pallas kernels: 62.9 us -> 61.5 us  [local(): pl.pallas_call(kernel, out_shape=(jax.ShapeDtypeStruct((24, 128), F32), j...]
where the time goes in v4:
time: 64.1 us; the launch traced here: 63.9 us
  Pallas kernels  63.3 us (99%)
    pallas_call x1, Pallas kernels, local(): pl.pallas_call(kernel, out_shape=(jax.ShapeDtypeStruct((24, 128), F32), j...  61.5 us
    pallas_call x1, Pallas kernels, local(): pl.pallas_call(finish, out_shape=(jax.ShapeDtypeStruct((8, 128), F32), ja...  1.82 us

profile of v4, /device:TPU:1, one launch (start us, length us, event | category | flops | bytes accessed | tf_op | source)
XLA Modules:
  0.0 63.9 jit_solution(2562413254780896094)
XLA Ops:
  0.6 61.5 %shard_map.75 = (f32[24,128]{1,0:T(8,128)}, f32[64,64]{1,0:T(8,128)}, f32[64,2048]{1,0:T(8,128)}) custom-call(f32[64,1024]{1,0:T(8,128)} %x_hbm.1, f32[64,2048]{1,0:T(8,128)} %y_hbm.1, f32[8,128]{1,0:T(8,128)} %bitcast.5, f32[16,128]{1,0:T(8,128)} %bitcast.4), custom_call_target="tpu_custom_call" | custom-call | tf_op jit(solution)/shard_map/pallas_call | solution.py:494
  62.1 1.8 %shard_map.76 = (f32[8,128]{1,0:T(8,128)}, f32[16,128]{1,0:T(8,128)}, f32[64,64]{1,0:T(8,128)}, f32[64,2048]{1,0:T(8,128)}) custom-call(f32[24,128]{1,0:T(8,128)} %get-tuple-element.11.fg, f32[64,64]{1,0:T(8,128)} %get-tuple-element.12.sm, f32[64,2048]{1,0:T(8,128)} %get-tuple-element.13.tm), custom_call_target="tpu_custom_call" | custom-call | tf_op jit(solution)/shard_map/pallas_call | solution.py:556

commit v5 on v4

--- a/solution.py
+++ b/solution.py
@@ -327,12 +327,12 @@
     gather_x(2)
 
     scatter_y(0)
-    scatter_y(1)
     g2y_in[0] = g2_out[...]
     await_bytes(g2y_in.at[pl.ds(1, 7)], recv.at[6])
     g2_mid[...] = jnp.sum(g2y_in[...], axis=0)
     for dx in X_OFFSETS:
         push(g2_mid, g2x_in.at[dx], 8, xy(0, dx))
+    scatter_y(1)
     scatter_y(2)
     await_bytes(by_in.at[pl.ds(1, 7)], recv.at[9])
     total = tn[3, own_rows, :]

time: 64.1 us -> 64.1 us (level)
  no operation moved by 1% of the time
where the time goes in v5:
time: 64.1 us; the launch traced here: 63.9 us
  Pallas kernels  63.3 us (99%)
    pallas_call x1, Pallas kernels, local(): pl.pallas_call(kernel, out_shape=(jax.ShapeDtypeStruct((24, 128), F32), j...  61.5 us
    pallas_call x1, Pallas kernels, local(): pl.pallas_call(finish, out_shape=(jax.ShapeDtypeStruct((8, 128), F32), ja...  1.82 us

profile of v5, /device:TPU:1, one launch (start us, length us, event | category | flops | bytes accessed | tf_op | source)
XLA Modules:
  0.0 63.9 jit_solution(4237484499178398908)
XLA Ops:
  0.6 61.5 %shard_map.75 = (f32[24,128]{1,0:T(8,128)}, f32[64,64]{1,0:T(8,128)}, f32[64,2048]{1,0:T(8,128)}) custom-call(f32[64,1024]{1,0:T(8,128)} %x_hbm.1, f32[64,2048]{1,0:T(8,128)} %y_hbm.1, f32[8,128]{1,0:T(8,128)} %bitcast.5, f32[16,128]{1,0:T(8,128)} %bitcast.4), custom_call_target="tpu_custom_call" | custom-call | tf_op jit(solution)/shard_map/pallas_call | solution.py:494
  62.1 1.8 %shard_map.76 = (f32[8,128]{1,0:T(8,128)}, f32[16,128]{1,0:T(8,128)}, f32[64,64]{1,0:T(8,128)}, f32[64,2048]{1,0:T(8,128)}) custom-call(f32[24,128]{1,0:T(8,128)} %get-tuple-element.11.fg, f32[64,64]{1,0:T(8,128)} %get-tuple-element.12.sm, f32[64,2048]{1,0:T(8,128)} %get-tuple-element.13.tm), custom_call_target="tpu_custom_call" | custom-call | tf_op jit(solution)/shard_map/pallas_call | solution.py:556
